TPU v7x, 32 devices: a whole 2x2x4 slice. The times are simulated.
32 devices in a mesh: dp: 2 (over y), seq: 16 (over z, x, core).
Axes of the slice: x: 2, y: 2, z: 4, core: 2. Of those that a mesh axis runs over, the one named last changes fastest.
Arguments:
- hidden_in: bfloat16 [8, 4096, 768], P('dp', 'seq'), may hold values from -6 to 6
- positions: int32 [8, 4096], P('dp', 'seq'), may hold values from 0 to 4095
- ln1_gain: float32 [768], replicated, may hold values from 0.5 to 1.5
- ln1_bias: float32 [768], replicated, may hold values from -4 to 4
- ln2_gain: float32 [768], replicated, may hold values from 0.5 to 1.5
- ln2_bias: float32 [768], replicated, may hold values from -4 to 4
- query_projection: bfloat16 [768, 768], replicated, may hold values from -0.3125 to 0.3125
- query_bias: float32 [768], replicated, may hold values from -4 to 4
- shared_key_weight: bfloat16 [768, 64], replicated, may hold values from -0.21875 to 0.21875
- shared_key_bias: float32 [64], replicated, may hold values from -4 to 4
- shared_value_weight: bfloat16 [768, 64], replicated, may hold values from -0.21875 to 0.21875
- shared_value_bias: float32 [64], replicated, may hold values from -4 to 4
- output_weight: bfloat16 [768, 768], replicated, may hold values from -0.625 to 0.625
- output_bias: float32 [768], replicated, may hold values from -4 to 4
- up_weight: bfloat16 [768, 3072], replicated, may hold values from -0.21875 to 0.21875
- up_bias: float32 [3072], replicated, may hold values from -4 to 4
- down_weight: bfloat16 [3072, 768], replicated, may hold values from -0.109375 to 0.109375
- down_bias: float32 [768], replicated, may hold values from -4 to 4
- cotangent: bfloat16 [8, 4096, 768], P('dp', 'seq'), may hold values from -6 to 6
Outputs:
- layer_out: float32 [8, 4096, 768], P('dp', 'seq')
- input_grad: float32 [8, 4096, 768], P('dp', 'seq')
- grad_ln1_gain: float32 [768], replicated
- grad_ln1_bias: float32 [768], replicated
- grad_ln2_gain: float32 [768], replicated
- grad_ln2_bias: float32 [768], replicated
- grad_w_query: float32 [768, 768], replicated
- grad_b_query: float32 [768], replicated
- grad_w_key: float32 [768, 64], replicated
- grad_b_key: float32 [64], replicated
- grad_w_value: float32 [768, 64], replicated
- grad_b_value: float32 [64], replicated
- grad_w_out: float32 [768, 768], replicated
- grad_b_out: float32 [768], replicated
- up_weight_gradient: float32 [768, 3072], replicated
- grad_b_up: float32 [3072], replicated
- grad_w_down: float32 [3072, 768], replicated
- grad_b_down: float32 [768], replicated
All inputs are finite; a program needn't handle non-finite values.
Results may differ from a plain program's by a relative error of at most 0.033.
Values may be sent and summed in bfloat16 or wider, within the bound.
A program may use at most 192 MiB of HBM per device.

v0:
```python
import math

import jax
import jax.numpy as jnp
from jax import lax
from jax.sharding import PartitionSpec as P

D = 768
HEADS = 12
HEAD_DIM = 64
ROT_DIMS = 16


def layer_norm(values, gain, bias):
    center = values - jnp.mean(values, axis=-1, keepdims=True)
    spread = jnp.mean(center * center, axis=-1, keepdims=True)
    return center * lax.rsqrt(spread + 1e-05) * gain + bias


def gelu_exact(values):
    return 0.5 * values * (1.0 + jax.scipy.special.erf(values * (1.0 / math.sqrt(2.0))))


def rotary(values, cosine, sine_part):
    halfway = cosine.shape[-1]
    first_half = values[..., :halfway]
    second_half = values[..., halfway : 2 * halfway]
    return jnp.concatenate(
        [
            first_half * cosine - second_half * sine_part,
            second_half * cosine + first_half * sine_part,
            values[..., 2 * halfway :],
        ],
        axis=-1,
    )


def angles_of(positions):
    halfway = ROT_DIMS // 2
    frequency = jnp.exp(
        jnp.arange(halfway).astype(jnp.float32) * (-2.0 * math.log(10000.0) / ROT_DIMS)
    )
    angle_all = positions.astype(jnp.float32)[..., None] * frequency
    return (jnp.cos(angle_all), jnp.sin(angle_all))


def masked_scores(query_rows, key_all, query_pos, key_begin, block_len, score_scale):
    key_rows = lax.dynamic_slice_in_dim(key_all, key_begin, block_len, 0)
    scores = (
        jnp.einsum("qhd,kd->hqk", query_rows, key_rows, preferred_element_type=jnp.float32)
        * score_scale
    )
    columns = key_begin + jnp.arange(block_len, dtype=jnp.int32)
    return (jnp.where(columns[None, None, :] <= query_pos[None, :, None], scores, -1e30), key_rows)


def add_rows(running, part_rows, row_begin):
    current = lax.dynamic_slice_in_dim(running, row_begin, part_rows.shape[0], 0)
    return lax.dynamic_update_slice_in_dim(running, current + part_rows, row_begin, 0)


def attend_forward(queries, key_all, value_every_token):
    length, heads_here, head_size = queries.shape
    block_len = min(512, length)
    score_scale = head_size ** (-0.5)

    def per_block(carried, block_index):
        row_begin = block_index * block_len
        query_rows = lax.dynamic_slice_in_dim(queries, row_begin, block_len, 0)
        query_pos = row_begin + jnp.arange(block_len, dtype=jnp.int32)

        def stats_step(key_step, loop_state):
            running_top, running_sum = loop_state
            scores, unused = masked_scores(
                query_rows, key_all, query_pos, key_step * block_len, block_len, score_scale
            )
            new_top = jnp.maximum(running_top, jnp.max(scores, axis=-1))
            new_sum = running_sum * jnp.exp(running_top - new_top) + jnp.sum(
                jnp.exp(scores - new_top[..., None]), axis=-1
            )
            return (new_top, new_sum)

        start_state = (
            jnp.full((heads_here, block_len), -1e30, jnp.float32),
            jnp.zeros((heads_here, block_len), jnp.float32),
        )
        running_top, running_sum = lax.fori_loop(0, block_index + 1, stats_step, start_state)
        log_total = running_top + jnp.log(running_sum)

        def accumulate(key_step, running):
            scores, unused = masked_scores(
                query_rows, key_all, query_pos, key_step * block_len, block_len, score_scale
            )
            prob_rows = jnp.exp(scores - log_total[..., None]).astype(jnp.bfloat16)
            value_rows = lax.dynamic_slice_in_dim(
                value_every_token, key_step * block_len, block_len, 0
            )
            return running + jnp.einsum(
                "hqk,kd->qhd", prob_rows, value_rows, preferred_element_type=jnp.float32
            )

        attended_values = lax.fori_loop(
            0,
            block_index + 1,
            accumulate,
            jnp.zeros((block_len, heads_here, head_size), jnp.float32),
        )
        return (carried, (attended_values, log_total))

    unused, (attended_values, log_total) = lax.scan(
        per_block, None, jnp.arange(length // block_len, dtype=jnp.int32)
    )
    return (attended_values.reshape(length, heads_here, head_size), log_total)


def attend_backward(queries, key_all, value_every_token, attended_values, log_total, grad_attended):
    length, heads_here, head_size = queries.shape
    block_len = min(512, length)
    block_count = length // block_len
    score_scale = head_size ** (-0.5)
    row_delta = jnp.sum(grad_attended.astype(jnp.float32) * attended_values, axis=-1)
    row_delta = row_delta.reshape(block_count, block_len, heads_here).transpose(0, 2, 1)

    def per_block(carried, pieces):
        block_index, block_total, block_delta = pieces
        row_begin = block_index * block_len
        query_rows = lax.dynamic_slice_in_dim(queries, row_begin, block_len, 0)
        grad_rows = lax.dynamic_slice_in_dim(grad_attended, row_begin, block_len, 0)
        query_pos = row_begin + jnp.arange(block_len, dtype=jnp.int32)

        def inner_step(key_step, loop_state):
            query_grad, key_grads, value_grads = loop_state
            key_begin = key_step * block_len
            scores, key_rows = masked_scores(
                query_rows, key_all, query_pos, key_begin, block_len, score_scale
            )
            prob_rows = jnp.exp(scores - block_total[..., None])
            value_rows = lax.dynamic_slice_in_dim(value_every_token, key_begin, block_len, 0)
            grad_prob = jnp.einsum(
                "qhd,kd->hqk", grad_rows, value_rows, preferred_element_type=jnp.float32
            )
            grad_scores = (prob_rows * (grad_prob - block_delta[..., None])).astype(jnp.bfloat16)
            query_grad = (
                query_grad
                + jnp.einsum(
                    "hqk,kd->qhd", grad_scores, key_rows, preferred_element_type=jnp.float32
                )
                * score_scale
            )
            key_part = (
                jnp.einsum(
                    "hqk,qhd->kd", grad_scores, query_rows, preferred_element_type=jnp.float32
                )
                * score_scale
            )
            value_part = jnp.einsum(
                "hqk,qhd->kd",
                prob_rows.astype(jnp.bfloat16),
                grad_rows,
                preferred_element_type=jnp.float32,
            )
            return (
                query_grad,
                add_rows(key_grads, key_part, key_begin),
                add_rows(value_grads, value_part, key_begin),
            )

        start_state = (
            jnp.zeros((block_len, heads_here, head_size), jnp.float32),
            carried[0],
            carried[1],
        )
        query_grad, key_grads, value_grads = lax.fori_loop(
            0, block_index + 1, inner_step, start_state
        )
        return ((key_grads, value_grads), query_grad)

    zero_rows = jnp.zeros((length, head_size), jnp.float32)
    indices = jnp.arange(block_count, dtype=jnp.int32)
    (key_grads, value_grads), query_grad = lax.scan(
        per_block, (zero_rows, zero_rows), (indices, log_total, row_delta)
    )
    return (query_grad.reshape(length, heads_here, head_size), key_grads, value_grads)


def local(
    hidden_in,
    positions,
    ln1_gain,
    ln1_bias,
    ln2_gain,
    ln2_bias,
    query_projection,
    query_bias,
    shared_key_weight,
    shared_key_bias,
    shared_value_weight,
    shared_value_bias,
    output_weight,
    output_bias,
    up_weight,
    up_bias,
    down_weight,
    down_bias,
    cotangent,
):
    groups = 4
    seq_count, local_len = (hidden_in.shape[0], hidden_in.shape[1])
    devices_seq = lax.axis_size("seq")
    per_group = HEADS // groups
    group_width = per_group * HEAD_DIM
    hidden = hidden_in.astype(jnp.float32)
    cosine, sine_all = angles_of(positions)
    cos_heads = cosine[:, None, :, None, :]
    sin_heads = sine_all[:, None, :, None, :]
    attention_normed_input, pull_a = jax.vjp(layer_norm, hidden, ln1_gain, ln1_bias)
    feedforward_normed_input, pull_m = jax.vjp(layer_norm, hidden, ln2_gain, ln2_bias)
    attention_normed_input = attention_normed_input.astype(jnp.bfloat16)
    feedforward_normed_input = feedforward_normed_input.astype(jnp.bfloat16)
    query_matrix = query_projection.reshape(D, groups, group_width)
    query_before_rotary = jnp.einsum(
        "abt,thi->ahbi", attention_normed_input, query_matrix, preferred_element_type=jnp.float32
    ) + query_bias.reshape(groups, 1, group_width)
    query_shaped = query_before_rotary.reshape(seq_count, groups, local_len, per_group, HEAD_DIM)
    query_send = (
        rotary(query_shaped, cos_heads, sin_heads)
        .astype(jnp.bfloat16)
        .reshape(devices_seq, local_len, group_width)
    )
    key_value_weight = jnp.concatenate([shared_key_weight, shared_value_weight], axis=1)
    key_value_bias = jnp.concatenate([shared_key_bias, shared_value_bias])
    kv_pre = (
        jnp.einsum(
            "mhu,up->mhp",
            attention_normed_input,
            key_value_weight,
            preferred_element_type=jnp.float32,
        )
        + key_value_bias
    )
    key_side = rotary(kv_pre[..., :HEAD_DIM], cosine, sine_all)
    kv_send = jnp.concatenate([key_side, kv_pre[..., HEAD_DIM:]], axis=-1).astype(jnp.bfloat16)
    kv_copies = jnp.broadcast_to(
        kv_send[:, None], (seq_count, groups, local_len, 2 * HEAD_DIM)
    ).reshape(devices_seq, local_len, 2 * HEAD_DIM)
    query_here, kv_both = (
        lax.all_to_all(query_send, "seq", split_axis=0, concat_axis=1, tiled=True),
        lax.all_to_all(kv_copies, "seq", split_axis=0, concat_axis=1, tiled=True),
    )
    kv_here = kv_both[0]
    length = query_here.shape[1]
    queries = query_here[0].reshape(length, per_group, HEAD_DIM)
    key_all = kv_here[:, :HEAD_DIM]
    value_every_token = kv_here[:, HEAD_DIM:]
    attended_values, log_total = attend_forward(queries, key_all, value_every_token)
    attended_send = attended_values.astype(jnp.bfloat16).reshape(1, length, group_width)
    attended_tok = lax.all_to_all(
        attended_send, "seq", split_axis=1, concat_axis=0, tiled=True
    ).reshape(seq_count, groups, local_len, group_width)
    out_weight = output_weight.reshape(groups, group_width, D)
    attention_output = (
        jnp.einsum("sgle,gef->slf", attended_tok, out_weight, preferred_element_type=jnp.float32)
        + output_bias
    )
    up_before_activation = (
        jnp.einsum(
            "aet,tn->aen", feedforward_normed_input, up_weight, preferred_element_type=jnp.float32
        )
        + up_bias
    )
    activated_hidden, pull_gelu = jax.vjp(gelu_exact, up_before_activation)
    activated_hidden = activated_hidden.astype(jnp.bfloat16)
    feedforward_output = (
        jnp.einsum("tpx,xe->tpe", activated_hidden, down_weight, preferred_element_type=jnp.float32)
        + down_bias
    )
    layer_out = hidden + attention_output + feedforward_output
    grad_b_down = jnp.sum(cotangent.astype(jnp.float32), axis=(0, 1))
    grad_w_down = jnp.einsum(
        "niq,niv->qv", activated_hidden, cotangent, preferred_element_type=jnp.float32
    )
    activation_gradient = jnp.einsum(
        "mvj,tj->mvt", cotangent, down_weight, preferred_element_type=jnp.float32
    )
    up_gradient = pull_gelu(activation_gradient)[0].astype(jnp.bfloat16)
    up_weight_gradient = jnp.einsum(
        "ubp,ubr->pr", feedforward_normed_input, up_gradient, preferred_element_type=jnp.float32
    )
    grad_b_up = jnp.sum(up_gradient.astype(jnp.float32), axis=(0, 1))
    feedforward_normed_gradient = jnp.einsum(
        "mvj,yj->mvy", up_gradient, up_weight, preferred_element_type=jnp.float32
    )
    grad_w_out = jnp.einsum(
        "sgle,slf->gef", attended_tok, cotangent, preferred_element_type=jnp.float32
    ).reshape(D, D)
    grad_attended_tok = jnp.einsum(
        "slf,gef->sgle", cotangent, out_weight, preferred_element_type=jnp.float32
    ).astype(jnp.bfloat16)
    grad_attended = lax.all_to_all(
        grad_attended_tok.reshape(devices_seq, local_len, group_width),
        "seq",
        split_axis=0,
        concat_axis=1,
        tiled=True,
    )
    grad_attended = grad_attended[0].reshape(length, per_group, HEAD_DIM)
    query_grad, key_grads, value_grads = attend_backward(
        queries, key_all, value_every_token, attended_values, log_total, grad_attended
    )
    query_back = lax.all_to_all(
        query_grad.astype(jnp.bfloat16).reshape(1, length, group_width),
        "seq",
        split_axis=1,
        concat_axis=0,
        tiled=True,
    )
    kv_part = jnp.concatenate([key_grads, value_grads], axis=-1)
    kv_returned = lax.all_to_all(
        kv_part[None].astype(jnp.bfloat16), "seq", split_axis=1, concat_axis=0, tiled=True
    ).astype(jnp.float32)
    kv_grad = jnp.sum(kv_returned.reshape(seq_count, groups, local_len, 2 * HEAD_DIM), axis=1)
    kv_grad_low = kv_grad.astype(jnp.bfloat16)
    key_pre_grad = rotary(
        kv_grad_low[..., :HEAD_DIM].astype(jnp.float32), cosine, -sine_all
    ).astype(jnp.bfloat16)
    key_value_raw_gradient = jnp.concatenate([key_pre_grad, kv_grad_low[..., HEAD_DIM:]], axis=-1)
    grad_kv_weight = jnp.einsum(
        "zmo,zmf->of",
        attention_normed_input,
        key_value_raw_gradient,
        preferred_element_type=jnp.float32,
    )
    grad_kv_bias = jnp.sum(key_value_raw_gradient.astype(jnp.float32), axis=(0, 1))
    query_turned = query_back.reshape(seq_count, groups, local_len, per_group, HEAD_DIM).astype(
        jnp.float32
    )
    query_raw_gradient = (
        rotary(query_turned, cos_heads, -sin_heads)
        .astype(jnp.bfloat16)
        .reshape(seq_count, groups, local_len, group_width)
    )
    grad_w_query = jnp.einsum(
        "afz,awfo->zwo",
        attention_normed_input,
        query_raw_gradient,
        preferred_element_type=jnp.float32,
    ).reshape(D, D)
    grad_b_query = jnp.sum(query_raw_gradient.astype(jnp.float32), axis=(0, 2)).reshape(D)
    grad_normed_a = jnp.einsum(
        "cvbt,rvt->cbr", query_raw_gradient, query_matrix, preferred_element_type=jnp.float32
    )
    grad_normed_a = grad_normed_a + jnp.einsum(
        "mwf,pf->mwp", key_value_raw_gradient, key_value_weight, preferred_element_type=jnp.float32
    )
    grad_hidden_a, grad_ln1_gain, grad_ln1_bias = pull_a(grad_normed_a)
    grad_hidden_m, grad_ln2_gain, grad_ln2_bias = pull_m(feedforward_normed_gradient)
    input_grad = cotangent.astype(jnp.float32) + grad_hidden_a + grad_hidden_m
    totals = lax.psum(
        (
            grad_ln1_gain,
            grad_ln1_bias,
            grad_ln2_gain,
            grad_ln2_bias,
            grad_w_query,
            grad_b_query,
            grad_kv_weight,
            grad_kv_bias,
            grad_w_out,
            up_weight_gradient,
            grad_b_up,
            grad_w_down,
            grad_b_down,
        ),
        ("dp", "seq"),
    )
    rest_totals = totals[:9]
    w_up_total, b_up_total, w_down_total, b_down_total = (
        totals[9],
        totals[10],
        totals[11],
        totals[12],
    )
    kv_weight_total = rest_totals[6]
    kv_bias_total = rest_totals[7]
    return (
        layer_out,
        input_grad,
        rest_totals[0],
        rest_totals[1],
        rest_totals[2],
        rest_totals[3],
        rest_totals[4],
        rest_totals[5],
        kv_weight_total[:, :HEAD_DIM],
        kv_bias_total[:HEAD_DIM],
        kv_weight_total[:, HEAD_DIM:],
        kv_bias_total[HEAD_DIM:],
        rest_totals[8],
        b_down_total,
        w_up_total,
        b_up_total,
        w_down_total,
        b_down_total,
    )


def solution(mesh):
    placed = (
        P("dp", "seq", None),
        P("dp", "seq"),
        P(),
        P(),
        P(),
        P(),
        P(),
        P(),
        P(),
        P(),
        P(),
        P(),
        P(),
        P(),
        P(),
        P(),
        P(),
        P(),
        P("dp", "seq", None),
    )
    return jax.shard_map(
        local,
        mesh=mesh,
        in_specs=placed,
        out_specs=(
            P("dp", "seq", None),
            P("dp", "seq", None),
            P(),
            P(),
            P(),
            P(),
            P(),
            P(),
            P(),
            P(),
            P(),
            P(),
            P(),
            P(),
            P(),
            P(),
            P(),
            P(),
        ),
        check_vma=False,
    )
```

profile of v0, /device:TPU:0, one launch (start us, length us, event | category | flops | bytes accessed | tf_op | source)
XLA Modules:
  0.0 1263.1 jit_solution(7733888452762843699)
XLA Ops:
  13.7 7.4 all-to-all-start.1
  28.7 15.4 %all-to-all-done.1 = bf16[16,256,128]{1,2,0:T(8,128)(2,1)} async-done(((bf16[16,256,128]{1,2,0:T(8,128)(2,1)}), bf16[16,256,128]{1,2,0:T(8,128)(2,1)}, u32[]{:S(2)}, u32[]{:S(2)}) %all-to-all-start.1) | async-done | bytes 1048608 | tf_op jit(solution)/shard_map/all_to_all | solution.py:248
  44.1 6.9 all-to-all-start
  60.7 22.3 %all-to-all-done = bf16[16,256,192]{1,2,0:T(8,128)(2,1)} async-done(((bf16[16,256,192]{1,2,0:T(8,128)(2,1)}), bf16[16,256,192]{1,2,0:T(8,128)(2,1)}, u32[]{:S(2)}, u32[]{:S(2)}) %all-to-all-start) | async-done | bytes 1572896 | tf_op jit(solution)/shard_map/all_to_all | solution.py:247
  83.1 9.7 all-to-all-start.3
  97.1 183.0 %while.75 = (s32[]{:T(128)}, f32[8,512,3,64]{1,3,2,0:T(8,128)}, f32[8,3,512]{2,1,0:T(4,128)}, s32[8]{0:T(128)S(1)}, bf16[4096,3,64]{0,2,1:T(8,128)(2,1)}, /*inde...) while((s32[]{:T(128)}, f32[8,512,3,64]{1,3,2,0:T(8,128)}, ...), condition=%wide.region_9.10_spmd.clone, body=%wide.region_2.9_spmd.sunk.clone | while | flops 311269888 | bytes 10696477 | solution.py:110
  127.0 7.1 while.74
  137.7 7.1 while.73
  145.4 9.4 while.74
  158.5 8.8 while.73
  168.0 11.8 while.74
  183.5 10.6 while.73
  194.7 14.2 %while.74 = (s32[]{:T(128)}, f32[512,3,64]{0,2,1:T(8,128)S(1)}, s32[]{:T(128)}, bf16[4096,64]{0,1:T(8,128)(2,1)}, bf16[4096,64]{0,1:T(8,128)(2,1)S(1)}, /*index=...) while((s32[]{:T(128)}, f32[512,3,64]{0,2,1:T(8,128)S(1)}, ...), condition=%wide.region_8.8_spmd.clone, body=%wide.region_7.7_spmd.clone.sunk | while | flops 204833792 | bytes 1655987 | solution.py:102
  212.5 12.4 while.73
  225.6 16.5 %while.74 = (s32[]{:T(128)}, f32[512,3,64]{0,2,1:T(8,128)S(1)}, s32[]{:T(128)}, bf16[4096,64]{0,1:T(8,128)(2,1)}, bf16[4096,64]{0,1:T(8,128)(2,1)S(1)}, /*index=...) while((s32[]{:T(128)}, f32[512,3,64]{0,2,1:T(8,128)S(1)}, ...), condition=%wide.region_8.8_spmd.clone, body=%wide.region_7.7_spmd.clone.sunk | while | flops 204833792 | bytes 1655987 | solution.py:102
  245.7 14.2 %while.73 = (s32[]{:T(128)}, f32[3,512]{1,0:T(4,128)S(1)}, f32[3,512]{1,0:T(4,128)S(1)}, s32[]{:T(128)}, bf16[4096,64]{0,1:T(8,128)(2,1)S(1)}, /*index=5*/bf16[5...) while((s32[]{:T(128)}, f32[3,512]{1,0:T(4,128)S(1)}, ...), condition=%wide.region_6.6_spmd.clone, body=%wide.region_3.5_spmd.clone.sunk | while | flops 106434568 | bytes 7428271 | solution.py:87
  260.5 18.9 %while.74 = (s32[]{:T(128)}, f32[512,3,64]{0,2,1:T(8,128)S(1)}, s32[]{:T(128)}, bf16[4096,64]{0,1:T(8,128)(2,1)}, bf16[4096,64]{0,1:T(8,128)(2,1)S(1)}, /*index=...) while((s32[]{:T(128)}, f32[512,3,64]{0,2,1:T(8,128)S(1)}, ...), condition=%wide.region_8.8_spmd.clone, body=%wide.region_7.7_spmd.clone.sunk | while | flops 204833792 | bytes 1655987 | solution.py:102
  300.5 276.7 %while.77 = (s32[]{:T(128)}, f32[4096,64]{0,1:T(8,128)S(1)}, f32[4096,64]{0,1:T(8,128)}, bf16[8,512,3,64]{1,3,2,0:T(8,128)(2,1)}, s32[8]{0:T(128)}, /*index=5*/b...) while((s32[]{:T(128)}, f32[4096,64]{0,1:T(8,128)S(1)}, ...), condition=%wide.region_14.15_spmd.clone, body=%wide.region_11.14_spmd.sunk.clone | while | flops 511738880 | bytes 19266168 | solution.py:180
  305.8 6.4 while.76
  318.1 12.8 %while.76 = (s32[]{:T(128)}, f32[512,3,64]{0,2,1:T(8,128)S(1)}, f32[4096,64]{0,1:T(8,128)S(1)}, f32[4096,64]{0,1:T(8,128)}, s32[]{:T(128)}, /*index=5*/bf16[4096...) while((s32[]{:T(128)}, f32[512,3,64]{0,2,1:T(8,128)S(1)}, ...), condition=%wide.region_13.13_spmd.clone, body=%wide.region_12.12_spmd.clone.sunk | while | flops 511738880 | bytes 17262824 | solution.py:173
  336.7 19.2 %while.76 = (s32[]{:T(128)}, f32[512,3,64]{0,2,1:T(8,128)S(1)}, f32[4096,64]{0,1:T(8,128)S(1)}, f32[4096,64]{0,1:T(8,128)}, s32[]{:T(128)}, /*index=5*/bf16[4096...) while((s32[]{:T(128)}, f32[512,3,64]{0,2,1:T(8,128)S(1)}, ...), condition=%wide.region_13.13_spmd.clone, body=%wide.region_12.12_spmd.clone.sunk | while | flops 511738880 | bytes 17262824 | solution.py:173
  361.7 25.5 %while.76 = (s32[]{:T(128)}, f32[512,3,64]{0,2,1:T(8,128)S(1)}, f32[4096,64]{0,1:T(8,128)S(1)}, f32[4096,64]{0,1:T(8,128)}, s32[]{:T(128)}, /*index=5*/bf16[4096...) while((s32[]{:T(128)}, f32[512,3,64]{0,2,1:T(8,128)S(1)}, ...), condition=%wide.region_13.13_spmd.clone, body=%wide.region_12.12_spmd.clone.sunk | while | flops 511738880 | bytes 17262824 | solution.py:173
  393.1 31.9 %while.76 = (s32[]{:T(128)}, f32[512,3,64]{0,2,1:T(8,128)S(1)}, f32[4096,64]{0,1:T(8,128)S(1)}, f32[4096,64]{0,1:T(8,128)}, s32[]{:T(128)}, /*index=5*/bf16[4096...) while((s32[]{:T(128)}, f32[512,3,64]{0,2,1:T(8,128)S(1)}, ...), condition=%wide.region_13.13_spmd.clone, body=%wide.region_12.12_spmd.clone.sunk | while | flops 511738880 | bytes 17262824 | solution.py:173
  430.8 38.3 %while.76 = (s32[]{:T(128)}, f32[512,3,64]{0,2,1:T(8,128)S(1)}, f32[4096,64]{0,1:T(8,128)S(1)}, f32[4096,64]{0,1:T(8,128)}, s32[]{:T(128)}, /*index=5*/bf16[4096...) while((s32[]{:T(128)}, f32[512,3,64]{0,2,1:T(8,128)S(1)}, ...), condition=%wide.region_13.13_spmd.clone, body=%wide.region_12.12_spmd.clone.sunk | while | flops 511738880 | bytes 17262824 | solution.py:173
  474.9 44.6 %while.76 = (s32[]{:T(128)}, f32[512,3,64]{0,2,1:T(8,128)S(1)}, f32[4096,64]{0,1:T(8,128)S(1)}, f32[4096,64]{0,1:T(8,128)}, s32[]{:T(128)}, /*index=5*/bf16[4096...) while((s32[]{:T(128)}, f32[512,3,64]{0,2,1:T(8,128)S(1)}, ...), condition=%wide.region_13.13_spmd.clone, body=%wide.region_12.12_spmd.clone.sunk | while | flops 511738880 | bytes 17262824 | solution.py:173
  525.4 51.0 %while.76 = (s32[]{:T(128)}, f32[512,3,64]{0,2,1:T(8,128)S(1)}, f32[4096,64]{0,1:T(8,128)S(1)}, f32[4096,64]{0,1:T(8,128)}, s32[]{:T(128)}, /*index=5*/bf16[4096...) while((s32[]{:T(128)}, f32[512,3,64]{0,2,1:T(8,128)S(1)}, ...), condition=%wide.region_13.13_spmd.clone, body=%wide.region_12.12_spmd.clone.sunk | while | flops 511738880 | bytes 17262824 | solution.py:173
  585.1 23.4 %reduce.4 = bf16[4096,128]{1,0:T(8,128)(2,1)} reduce(bf16[4096,1,128]{2,1,0:T(2,128)(2,1)S(1)} %bitcast.309, bf16[]{:T(256)} %broadcast.286), dimensions={1}, to_apply=%bitcast.192.reduce_sub_computation | reduce | bytes 2097154
  610.6 6.4 all-to-all-start.5
  622.1 9.8 copy.226
  631.9 25.0 %reduce.3 = bf16[4096,192]{1,0:T(8,128)(2,1)} reduce(bf16[4096,1,192]{2,1,0:T(2,128)(2,1)} %bitcast.302, bf16[]{:T(256)} %broadcast.286), dimensions={1}, to_apply=%bitcast.190.reduce_sub_computation | reduce | bytes 3145730
  662.4 6.4 all-to-all-start.2
  668.9 10.9 multiply_convert_fusion
  679.8 13.1 %convert_reduce_fusion = (f32[3072]{0:T(1024)}, bf16[4,256,3072]{2,1,0:T(8,128)(2,1)}) fusion(bf16[4,256,768]{2,1,0:T(8,128)(2,1)S(1)} %copy-done.9, bf16[3072,768]{1,0:T(8,128)(2,1)} %param.45, f32[4,256,3072]{2,1,0:T(8,128)S(1)} %get-tuple-element.676, f32[3072]{0:T(1024)S(1)} %copy-done.38), kind=kOutput, calls=%fused_computation.75 | convolution fusion | flops 4882166784 | bytes 25190400 | tf_op jit(solution)/shard_map/mvj,tj->mvt/dot_general | solution.py:282
  698.6 9.8 copy.237
  708.5 25.0 %reduce.5 = bf16[4096,192]{1,0:T(8,128)(2,1)} reduce(bf16[4096,1,192]{2,1,0:T(2,128)(2,1)} %bitcast.301, bf16[]{:T(256)} %broadcast.286), dimensions={1}, to_apply=%bitcast.188.reduce_sub_computation | reduce | bytes 3145730
  738.9 6.2 all-to-all-start.4
  745.1 11.2 convolution_bitcast_fusion.2
  756.2 10.1 convolution_bitcast_fusion.1
  785.5 10.7 reshape.402
  796.2 9.6 copy.227
  809.7 10.7 reshape.400
  820.4 9.6 copy.238
  848.2 9.7 fusion.68
  857.9 9.8 fusion.70
  879.7 43.5 %all-reduce = (f32[768]{0:T(1024)}, f32[768]{0:T(1024)}, f32[768]{0:T(1024)}, f32[768]{0:T(1024)}, f32[768]{0:T(1024)}, /*index=5*/f32[128]{0:T(128)S(1)}, f32[768]{0:T(1024)S(1)}, f32[3072]{0:T(1024)}) all-reduce(f32[768]{0:T(1024)S(1)} %get-tuple-element.525, ...), channel_id=1, replica_groups=mesh['dp'=2,'seq'=16] {'dp','seq'}, use_global_device_ids=true, to_apply=%region_21.22 | all-reduce | flops 7808 | bytes 62464 | tf_op jit(solution)/shard_map/psum | solution.py:358
  923.8 6.2 fusion.88
  930.1 301.8 %all-reduce.4.cloned.1.call-done = (f32[768,768]{1,0:T(8,128)}, f32[768,128]{1,0:T(8,128)}, f32[768,768]{1,0:T(8,128)}, f32[768,3072]{1,0:T(8,128)}, f32[3072,768]{1,0:T(8,128)}) async-done(((f32[768,768]{1,0:T(8,128)}, f32[768,128]{1,0:T(8,128)}, f32[768,768]{1,0:T(8,128)}, f32[768,3072]{1,0:T(8,128)}, f32[3072,768]{1,0:T(8,128)}), (f32[768,768]{1,0:T(8,128)}, f32[768,128]{1,0:T(8,128)}, ...) | async-done | bytes 23986192 | tf_op jit(solution)/shard_map/psum | solution.py:358
  1243.0 9.3 copy.362
  (919 shorter events, 598.6 us)
Async XLA Ops:
  7.2 43.9 %copy-start = (bf16[768,768]{1,0:T(8,128)(2,1)S(1)}, bf16[768,768]{1,0:T(8,128)(2,1)}, u32[]{:S(2)}) copy-start(bf16[768,768]{1,0:T(8,128)(2,1)} %param.41) | copy-start | bytes 3538948
  7.2 4.1 copy-start.1
  7.2 4.0 copy-start.32
  7.2 4.0 copy-start.44
  7.2 4.0 copy-start.45
  7.2 4.1 copy-start.40
  7.3 4.1 copy-start.23
  7.3 4.1 copy-start.18
  7.3 4.1 copy-start.20
  7.3 5.0 copy-start.35
  9.2 14.4 %copy-start.16 = (f32[4,256]{1,0:T(4,128)}, f32[4,256]{1,0:T(4,128)S(1)}, u32[]{:S(2)}) copy-start(f32[4,256]{1,0:T(4,128)S(1)} %broadcast_multiply_fusion) | copy-start | bytes 12292
  11.2 12.4 copy-start.25
  12.6 10.9 copy-start.33
  13.7 30.4 %all-to-all-start.1 = ((bf16[16,256,128]{1,2,0:T(8,128)(2,1)}), bf16[16,256,128]{1,2,0:T(8,128)(2,1)}, u32[]{:S(2)}, u32[]{:S(2)}) async-start(bf16[16,256,128]{1,2,0:T(8,128)(2,1)} %bitcast.312), calls=%async_computation.1 | async-start | bytes 2097152 | tf_op jit(solution)/shard_map/all_to_all | solution.py:248
  27.3 23.7 %copy-start.8 = (bf16[4,256,768]{2,1,0:T(8,128)(2,1)S(1)}, bf16[4,256,768]{2,1,0:T(8,128)(2,1)}, u32[]{:S(2)}) copy-start(bf16[4,256,768]{2,1,0:T(8,128)(2,1)} %param.47) | copy-start | bytes 4718596
  44.1 39.0 %all-to-all-start = ((bf16[16,256,192]{1,2,0:T(8,128)(2,1)}), bf16[16,256,192]{1,2,0:T(8,128)(2,1)}, u32[]{:S(2)}, u32[]{:S(2)}) async-start(bf16[16,256,192]{1,2,0:T(8,128)(2,1)} %bitcast.16), calls=%async_computation | async-start | bytes 3145728 | tf_op jit(solution)/shard_map/all_to_all | solution.py:247
  83.1 197.1 %all-to-all-start.3 = ((bf16[16,256,192]{1,2,0:T(8,128)(2,1)}), bf16[16,256,192]{1,2,0:T(8,128)(2,1)}, u32[]{:S(2)}, u32[]{:S(2)}) async-start(bf16[16,256,192]{1,2,0:T(8,128)(2,1)} %bitcast.30), calls=%async_computation.3 | async-start | bytes 3145728 | tf_op jit(solution)/shard_map/all_to_all | solution.py:299
  610.6 51.8 %all-to-all-start.5 = ((bf16[16,2,16384]{2,1,0:T(2,128)(2,1)}), bf16[16,2,16384]{2,1,0:T(2,128)(2,1)}, u32[]{:S(2)}, u32[]{:S(2)}) async-start(bf16[16,2,16384]{2,1,0:T(2,128)(2,1)} %reshape.403), calls=%async_computation.5 | async-start | bytes 2097152 | tf_op jit(solution)/shard_map/all_to_all | solution.py:318
  656.9 12.0 copy-start.2
  656.9 12.0 copy-start.17
  656.9 12.0 copy-start.22
  656.9 12.0 copy-start.26
  656.9 12.0 copy-start.38
  656.9 12.0 copy-start.39
  662.4 76.4 %all-to-all-start.2 = ((bf16[16,2,24576]{2,1,0:T(2,128)(2,1)}), bf16[16,2,24576]{2,1,0:T(2,128)(2,1)}, u32[]{:S(2)}, u32[]{:S(2)}) async-start(bf16[16,2,24576]{2,1,0:T(2,128)(2,1)} %reshape.401), calls=%async_computation.2 | async-start | bytes 3145728 | tf_op jit(solution)/shard_map/all_to_all | solution.py:257
  668.9 10.9 copy-start.9
  679.8 13.1 %copy-start.4 = (bf16[8,512,3,64]{1,3,2,0:T(8,128)(2,1)S(1)}, bf16[8,512,3,64]{1,3,2,0:T(8,128)(2,1)}, u32[]{:S(2)}) copy-start(bf16[8,512,3,64]{1,3,2,0:T(8,128)(2,1)} %get-tuple-element.264) | copy-start | bytes 4718596
  738.9 70.8 %all-to-all-start.4 = ((bf16[16,2,24576]{2,1,0:T(2,128)(2,1)}), bf16[16,2,24576]{2,1,0:T(2,128)(2,1)}, u32[]{:S(2)}, u32[]{:S(2)}) async-start(bf16[16,2,24576]{2,1,0:T(2,128)(2,1)} %reshape.399), calls=%async_computation.4 | async-start | bytes 3145728 | tf_op jit(solution)/shard_map/all_to_all | solution.py:310
  745.0 486.9 %all-reduce.4.cloned.1.call-start = ((), (), s32[]{:S(2)}) async-start(), calls=%async_computation.6 | async-start | bytes 47972352 | tf_op jit(solution)/shard_map/psum | solution.py:358
  745.1 11.2 copy-start.10
  772.1 4.5 copy-start.30
  772.1 4.5 copy-start.36
  772.1 10.9 copy-start.24
  830.0 7.3 copy-start.14
  830.0 7.3 copy-start.15
  840.7 3.3 copy-start.7
  867.8 3.4 copy-start.3
  867.8 3.4 copy-start.19
  867.8 3.4 copy-start.21
  876.1 3.6 copy-start.31
  876.1 3.6 copy-start.37
  876.1 47.7 %copy-start.42 = (f32[768]{0:T(1024)S(1)}, f32[768]{0:T(1024)}, u32[]{:S(2)}) copy-start(f32[768]{0:T(1024)} %param.46) | copy-start | bytes 9220
  876.2 47.7 %copy-start.43 = (f32[768]{0:T(1024)S(1)}, f32[768]{0:T(1024)}, u32[]{:S(2)}) copy-start(f32[768]{0:T(1024)} %param.42) | copy-start | bytes 9220
  923.2 314.6 %copy-start.34 = (f32[768]{0:T(1024)}, f32[768]{0:T(1024)S(1)}, u32[]{:S(2)}) copy-start(f32[768]{0:T(1024)S(1)} %get-tuple-element.1426) | copy-start | bytes 9220
  1234.0 7.6 copy-start.6
  1241.6 10.7 slice-start
  1243.0 9.3 slice-start.1
  1243.0 9.3 slice-start.2
  (8 other events, 14.6 us)
Sparse Core Ops, SparseCore 0:
  848.3 383.4 all-reduce.3
where the time goes:
time: 1280 us; the launch traced here: 1260 us
  matrix products  413 us (32%)
  waiting for transfers between devices  340 us (27%)
  local copies, waits for them, and re-layouts  224 us (18%)
  other arithmetic  158 us (12%)
  blocking collectives  43.5 us (3%)
  starting transfers between devices  43 us (3%)
  loops' own time  27.3 us (2%)
  between operations  15.1 us (1%)
    psum x1, waiting for transfers between devices, local(): lax.psum((grad_ln1_gain, grad_ln1_bias, grad_ln2_gain, grad_ln2_bias, gra...  302 us
    dot_general x36, matrix products, inner_step(): jnp.einsum('hqk,qhd->kd', prob_rows.astype(jnp.bfloat16), grad_rows, pref...  91 us
    dot_general x36, matrix products, accumulate(): jnp.einsum('hqk,kd->qhd', prob_rows, value_rows, preferred_element_type=j...  75.4 us
    unnamed x5, other arithmetic  74.6 us
    dot_general x36, matrix products, inner_step(): jnp.einsum('qhd,kd->hqk', grad_rows, value_rows, preferred_element_type=j...  71.8 us
    unnamed x115, local copies, waits for them, and re-layouts  69.4 us
    dot_general x72, matrix products, masked_scores(): jnp.einsum('qhd,kd->hqk', query_rows, key_rows, preferred_element_type=jn...  48.6 us
    psum x1, blocking collectives, local(): lax.psum((grad_ln1_gain, grad_ln1_bias, grad_ln2_gain, grad_ln2_bias, gra...  43.5 us
  transfers between devices with their start and end apart: 7, of which 3 were waited for; matrix products, arithmetic and copies ran while one was open for 32% of the time, Pallas kernels for 0%

commit v1 on v0

v1 whole, which is shorter than its diff:
```python
import math

import jax
import jax.numpy as jnp
from jax import lax
from jax.experimental import pallas as pl
from jax.experimental.pallas import tpu as pltpu
from jax.sharding import PartitionSpec as P

D = 768
HEADS = 12
HEAD_DIM = 64
ROT_DIMS = 16
BF = jnp.bfloat16
F32 = jnp.float32
LOG2E = math.log2(math.e)
TILE = 256


def layer_norm(values, gain, bias):
    center = values - jnp.mean(values, axis=-1, keepdims=True)
    spread = jnp.mean(center * center, axis=-1, keepdims=True)
    return center * lax.rsqrt(spread + 1e-05) * gain + bias


def gelu_exact(values):
    return 0.5 * values * (1.0 + jax.scipy.special.erf(values * (1.0 / math.sqrt(2.0))))


def rotary_rows(values, cosine, sine):
    half = cosine.shape[-2]
    first, second = values[..., :half, :], values[..., half : 2 * half, :]
    return jnp.concatenate(
        [first * cosine - second * sine, second * cosine + first * sine, values[..., 2 * half :, :]],
        axis=-2,
    )


def angles_of(positions):
    half = ROT_DIMS // 2
    frequency = jnp.exp(
        jnp.arange(half).astype(F32) * (-2.0 * math.log(10000.0) / ROT_DIMS)
    )
    angle = positions.astype(F32)[:, None, :] * frequency[None, :, None]
    return jnp.cos(angle), jnp.sin(angle)


def dot(a, b, ca, cb):
    return lax.dot_general(a, b, (((ca,), (cb,)), ((), ())), preferred_element_type=F32)


def attention_kernel(
    q_ref, g_ref, k_ref, v_ref, kt_ref, vt_ref, o_ref, dq_ref, dk_ref, dv_ref, s_ref, p_ref
):
    tiles, width, rows = q_ref.shape
    heads = width // HEAD_DIM
    lanes = heads * rows
    block = rows
    dk_ref[...] = jnp.zeros_like(dk_ref)
    dv_ref[...] = jnp.zeros_like(dv_ref)
    keep = lax.broadcasted_iota(jnp.int32, (block, rows), 0) <= lax.broadcasted_iota(
        jnp.int32, (block, rows), 1
    )
    keep = jnp.concatenate([keep] * heads, axis=1)

    def side(ref, j):
        return jnp.concatenate(
            [ref[j, HEAD_DIM * h : HEAD_DIM * (h + 1), :] for h in range(heads)], axis=1
        )

    def at(kb):
        return pl.ds(pl.multiple_of(kb * block, block), block)

    def tile(step, carry):
        j = tiles - 1 - step
        q = side(q_ref, j)
        g = side(g_ref, j)

        def scores(kb, top):
            s = dot(k_ref[at(kb), :], q, 1, 0)
            s_ref[at(kb), :] = s
            return jnp.maximum(top, jnp.max(s, axis=0, keepdims=True))

        s = jnp.where(keep, dot(k_ref[at(j), :], q, 1, 0), -1e30)
        s_ref[at(j), :] = s
        top = lax.fori_loop(0, j, scores, jnp.max(s, axis=0, keepdims=True))

        def forward(kb, state):
            total, out = state
            p = jnp.exp2(s_ref[at(kb), :] - top)
            low = p.astype(BF)
            p_ref[at(kb), :] = low
            return (
                total + jnp.sum(p, axis=0, keepdims=True),
                out + dot(vt_ref[:, at(kb)], low, 1, 0),
            )

        total, out = lax.fori_loop(
            0,
            j + 1,
            forward,
            (jnp.zeros((1, lanes), F32), jnp.zeros((HEAD_DIM, lanes), F32)),
        )
        inverse = 1.0 / total
        out = out * inverse
        scaled = (g.astype(F32) * inverse).astype(BF)
        delta = jnp.sum(scaled.astype(F32) * out, axis=0, keepdims=True)
        high = delta.astype(BF)
        rest = delta - high.astype(F32)
        middle = rest.astype(BF)
        last = (rest - middle.astype(F32)).astype(BF)
        stacked = jnp.concatenate(
            [scaled, high, middle, last, jnp.zeros((13, lanes), BF)], axis=0
        )
        for h in range(heads):
            o_ref[j, HEAD_DIM * h : HEAD_DIM * (h + 1), :] = out[
                :, h * rows : (h + 1) * rows
            ].astype(BF)

        def backward(kb, dq):
            p = p_ref[at(kb), :]
            dp = dot(v_ref[at(kb), :], stacked, 1, 0)
            ds = (p.astype(F32) * dp).astype(BF)
            dv_ref[at(kb), :] += dot(p, scaled, 1, 1)
            dk_ref[at(kb), :] += dot(ds, q, 1, 1)
            return dq + dot(kt_ref[:, at(kb)], ds, 1, 0)

        dq = lax.fori_loop(0, j + 1, backward, jnp.zeros((HEAD_DIM, lanes), F32))
        dq = dq * (HEAD_DIM**-0.5)
        for h in range(heads):
            dq_ref[j, HEAD_DIM * h : HEAD_DIM * (h + 1), :] = dq[
                :, h * rows : (h + 1) * rows
            ].astype(BF)
        return carry

    lax.fori_loop(0, tiles, tile, 0)


def attention(q, g, key, value):
    tiles, width, rows = q.shape
    length = tiles * rows
    lanes = width // HEAD_DIM * rows
    ones = jnp.concatenate([jnp.full((length, 3), -1, BF), jnp.zeros((length, 13), BF)], axis=1)
    whole = pl.BlockSpec(memory_space=pltpu.VMEM)
    flops = 12 * length * length // 2 * width
    return pl.pallas_call(
        attention_kernel,
        out_shape=[jax.ShapeDtypeStruct(q.shape, BF)] * 2
        + [jax.ShapeDtypeStruct((length, HEAD_DIM), F32)] * 2,
        in_specs=[whole] * 6,
        out_specs=[whole] * 4,
        scratch_shapes=[pltpu.VMEM((length, lanes), F32), pltpu.VMEM((length, lanes), BF)],
        compiler_params=pltpu.CompilerParams(vmem_limit_bytes=56 * 2**20),
        cost_estimate=pl.CostEstimate(
            flops=6 * flops, bytes_accessed=4 * q.size, transcendentals=length * length // 2 * 3
        ),
        name="attention",
    )(q, g, key, jnp.concatenate([value, ones], axis=1), key.T, value.T)


def local(
    hidden_in,
    positions,
    ln1_gain,
    ln1_bias,
    ln2_gain,
    ln2_bias,
    query_projection,
    query_bias,
    shared_key_weight,
    shared_key_bias,
    shared_value_weight,
    shared_value_bias,
    output_weight,
    output_bias,
    up_weight,
    up_bias,
    down_weight,
    down_bias,
    cotangent,
):
    seq_count, local_len = hidden_in.shape[0], hidden_in.shape[1]
    ring = lax.axis_size("seq")
    groups = ring // seq_count
    per_group = HEADS // groups
    width = per_group * HEAD_DIM
    length = ring * local_len
    hidden = hidden_in.astype(F32)
    cosine, sine = angles_of(positions)
    normed_a, pull_a = jax.vjp(layer_norm, hidden, ln1_gain, ln1_bias)
    normed_m, pull_m = jax.vjp(layer_norm, hidden, ln2_gain, ln2_bias)
    normed_a = normed_a.astype(BF)
    normed_m = normed_m.astype(BF)

    def swap(x):
        return lax.all_to_all(x, "seq", split_axis=0, concat_axis=0, tiled=True)

    kv_weight = jnp.concatenate([shared_key_weight, shared_value_weight], axis=1)
    kv_bias = jnp.concatenate([shared_key_bias, shared_value_bias])
    kv_pre = jnp.einsum("stc,cw->swt", normed_a, kv_weight, preferred_element_type=F32)
    kv_pre = kv_pre + kv_bias[:, None]
    kv_low = jnp.concatenate(
        [rotary_rows(kv_pre[:, :HEAD_DIM], cosine, sine), kv_pre[:, HEAD_DIM:]], axis=1
    ).astype(BF)
    kv_send = jnp.broadcast_to(
        kv_low[:, None], (seq_count, groups, 2 * HEAD_DIM, local_len)
    ).reshape(ring, 2 * HEAD_DIM, local_len)
    query_pre = jnp.einsum("stc,cw->swt", normed_a, query_projection, preferred_element_type=F32)
    query_pre = (query_pre + query_bias[:, None]).reshape(seq_count, HEADS, HEAD_DIM, local_len)
    query_low = (rotary_rows(query_pre, cosine[:, None], sine[:, None]) * (LOG2E / 8.0)).astype(BF)
    query_send = query_low.reshape(ring, width, local_len)
    grad_attended = jnp.einsum(
        "stc,wc->swt", cotangent, output_weight, preferred_element_type=F32
    ).astype(BF)
    grad_send = grad_attended.reshape(ring, width, local_len)
    query_send, kv_send, grad_send = lax.optimization_barrier((query_send, kv_send, grad_send))
    kv_here = swap(kv_send)
    query_here = swap(query_send)
    grad_here = swap(grad_send)

    up_pre = jnp.einsum("stc,cf->stf", normed_m, up_weight, preferred_element_type=F32) + up_bias
    activation, pull_gelu = jax.vjp(gelu_exact, up_pre)
    activation = activation.astype(BF)
    feedforward = jnp.einsum(
        "stf,fc->stc", activation, down_weight, preferred_element_type=F32
    )
    activation_gradient = jnp.einsum(
        "stc,fc->stf", cotangent, down_weight, preferred_element_type=F32
    )
    grad_up = pull_gelu(activation_gradient)[0].astype(BF)
    grad_w_down = jnp.einsum(
        "stf,stc->fc", activation, cotangent, preferred_element_type=F32
    ).astype(BF)
    grad_w_up = jnp.einsum("stc,stf->cf", normed_m, grad_up, preferred_element_type=F32).astype(BF)
    grad_normed_m = jnp.einsum("stf,cf->stc", grad_up, up_weight, preferred_element_type=F32)
    grad_w_up, grad_w_down = lax.psum((grad_w_up, grad_w_down), ("dp", "seq"))
    grad_b_up = jnp.sum(grad_up.astype(F32), axis=(0, 1))
    grad_b_down = jnp.sum(cotangent.astype(F32), axis=(0, 1))

    def to_tiles(x):
        tile_len = max(TILE, local_len)
        x = x.reshape(length // tile_len, tile_len // local_len, width, local_len)
        return x.transpose(0, 2, 1, 3).reshape(length // tile_len, width, tile_len)

    def from_tiles(x):
        tile_len = max(TILE, local_len)
        x = x.reshape(length // tile_len, width, tile_len // local_len, local_len)
        return x.transpose(0, 2, 1, 3).reshape(ring, width, local_len)

    kv_rows = kv_here.transpose(0, 2, 1).reshape(length, 2 * HEAD_DIM)
    out, dq, dk, dv = attention(
        to_tiles(query_here), to_tiles(grad_here), kv_rows[:, :HEAD_DIM], kv_rows[:, HEAD_DIM:]
    )
    attended = swap(from_tiles(out)).reshape(seq_count, D, local_len)
    query_back = swap(from_tiles(dq)).reshape(seq_count, HEADS, HEAD_DIM, local_len)
    kv_part = jnp.concatenate([dk * (1.0 / LOG2E), dv], axis=1).astype(BF)
    kv_back = swap(kv_part.reshape(ring, local_len, 2 * HEAD_DIM)).astype(F32)
    kv_grad = jnp.sum(kv_back.reshape(seq_count, groups, local_len, 2 * HEAD_DIM), axis=1)
    kv_grad = kv_grad.astype(BF).astype(F32).transpose(0, 2, 1)

    attention_out = jnp.einsum(
        "swt,wc->stc", attended, output_weight, preferred_element_type=F32
    )
    layer_out = hidden + attention_out + feedforward + (output_bias + down_bias)
    grad_w_out = jnp.einsum("swt,stc->wc", attended, cotangent, preferred_element_type=F32)

    kv_raw = jnp.concatenate(
        [rotary_rows(kv_grad[:, :HEAD_DIM], cosine, -sine), kv_grad[:, HEAD_DIM:]], axis=1
    ).astype(BF)
    query_raw = (
        rotary_rows(query_back.astype(F32), cosine[:, None], -sine[:, None])
        .astype(BF)
        .reshape(seq_count, D, local_len)
    )
    raw = jnp.concatenate([query_raw, kv_raw], axis=1)
    weight = jnp.concatenate([query_projection, kv_weight], axis=1)
    grad_w_qkv = jnp.einsum("stc,swt->cw", normed_a, raw, preferred_element_type=F32)
    grad_b_qkv = jnp.sum(raw.astype(F32), axis=(0, 2))
    grad_normed_a = jnp.einsum("swt,cw->stc", raw, weight, preferred_element_type=F32)
    grad_hidden_a, grad_ln1_gain, grad_ln1_bias = pull_a(grad_normed_a)
    grad_hidden_m, grad_ln2_gain, grad_ln2_bias = pull_m(grad_normed_m)
    input_grad = cotangent.astype(F32) + grad_hidden_a + grad_hidden_m

    vectors = jnp.concatenate(
        [
            grad_ln1_gain,
            grad_ln1_bias,
            grad_ln2_gain,
            grad_ln2_bias,
            grad_b_qkv,
            grad_b_up,
            grad_b_down,
        ]
    )
    rest = jnp.concatenate(
        [grad_w_qkv, grad_w_out],
        axis=1,
    ).astype(BF)
    rest, grad_w_up, grad_w_down = lax.optimization_barrier((rest, grad_w_up, grad_w_down))
    rest, vectors = lax.psum((rest, vectors), ("dp", "seq"))
    rest = rest.astype(F32)
    qkv = D + 2 * HEAD_DIM
    ff = up_weight.shape[1]
    b_qkv = vectors[4 * D : 4 * D + qkv]
    b_up = vectors[4 * D + qkv : 4 * D + qkv + ff]
    b_down = vectors[4 * D + qkv + ff :]
    return (
        layer_out,
        input_grad,
        vectors[:D],
        vectors[D : 2 * D],
        vectors[2 * D : 3 * D],
        vectors[3 * D : 4 * D],
        rest[:, :D],
        b_qkv[:D],
        rest[:, D : D + HEAD_DIM],
        b_qkv[D : D + HEAD_DIM],
        rest[:, D + HEAD_DIM : qkv],
        b_qkv[D + HEAD_DIM :],
        rest[:, qkv:],
        b_down,
        grad_w_up.astype(F32),
        b_up,
        grad_w_down.astype(F32),
        b_down,
    )


def solution(mesh):
    rows = P("dp", "seq", None)
    placed = (rows, P("dp", "seq")) + (P(),) * 16 + (rows,)
    return jax.shard_map(
        local,
        mesh=mesh,
        in_specs=placed,
        out_specs=(rows, rows) + (P(),) * 16,
        check_vma=False,
    )
```

time: 1280 us -> 744 us (0.58)
  matrix products: 413 us -> 89.3 us
  local copies, waits for them, and re-layouts: 224 us -> 27.7 us
  Pallas kernels: 0 us -> 143 us
  other arithmetic: 158 us -> 41.5 us
  waiting for transfers between devices: 340 us -> 298 us
  blocking collectives: 43.5 us -> 72.6 us
  loops' own time: 27.3 us -> 0 us
    dot_general x267 -> x13, matrix products: 413 us -> 89.3 us  [the longest x1 15.2 us: local(): jnp.einsum('stc,fc->stf', cotangent, down_weight, preferred_element_type=...]
    pallas_call x0 -> x1, Pallas kernels: none -> 143 us  [attention(): pl.pallas_call(attention_kernel, out_shape=[jax.ShapeDtypeStruct(q.shape,...]
    psum x1 -> x2, waiting for transfers between devices: 302 us -> 221 us  [the longest x1 150 us: local(): grad_w_up, grad_w_down = lax.psum((grad_w_up, grad_w_down), ('dp', 'seq'))]
    unnamed x5 -> x2, other arithmetic: 74.6 us -> 0.01 us
    unnamed x115 -> x95, local copies, waits for them, and re-layouts: 69.4 us -> 4.44 us
    convert_element_type x11 -> x1, local copies, waits for them, and re-layouts: 44.1 us -> 2.58 us  [local(): query_raw = rotary_rows(query_back.astype(F32), cosine[:, None], -sine[:,...]
    all_to_all x6 -> x5, waiting for transfers between devices: 37.8 us -> 76.9 us  [swap(): return lax.all_to_all(x, 'seq', split_axis=0, concat_axis=0, tiled=True)]
    dynamic_slice x40 -> x0, local copies, waits for them, and re-layouts: 37.1 us -> none  [the longest x16 14.6 us: attend_forward(): lax.scan(per_block, None, jnp.arange(length // block_len, dtype=jnp.int32))]
  transfers between devices with their start and end apart: 7 -> 7, of which waited for: 3 -> 7; matrix products, arithmetic and copies ran while one was open for 32% -> 17% of each run, Pallas kernels for 0% -> 0%
where the time goes in v1:
time: 744 us; the launch traced here: 735 us
  waiting for transfers between devices  298 us (40%)
  Pallas kernels  143 us (19%)
  matrix products  89.3 us (12%)
  blocking collectives  72.6 us (10%)
  starting transfers between devices  47.9 us (6%)
  other arithmetic  41.5 us (6%)
  local copies, waits for them, and re-layouts  27.7 us (4%)
  between operations  15.2 us (2%)
    psum x1, waiting for transfers between devices, local(): grad_w_up, grad_w_down = lax.psum((grad_w_up, grad_w_down), ('dp', 'seq'))  150 us
    pallas_call x1, Pallas kernels, attention(): pl.pallas_call(attention_kernel, out_shape=[jax.ShapeDtypeStruct(q.shape,...  143 us
    all_to_all x5, waiting for transfers between devices, swap(): return lax.all_to_all(x, 'seq', split_axis=0, concat_axis=0, tiled=True)  76.9 us
    psum x1, waiting for transfers between devices, local(): rest, vectors = lax.psum((rest, vectors), ('dp', 'seq'))  71 us
    all_to_all x5, starting transfers between devices, swap(): return lax.all_to_all(x, 'seq', split_axis=0, concat_axis=0, tiled=True)  47.6 us
    psum x1, blocking collectives, local(): rest, vectors = lax.psum((rest, vectors), ('dp', 'seq'))  40.5 us
    all_to_all x1, blocking collectives, swap(): return lax.all_to_all(x, 'seq', split_axis=0, concat_axis=0, tiled=True)  32.1 us
    dot_general x1, matrix products, local(): jnp.einsum('stc,fc->stf', cotangent, down_weight, preferred_element_type=...  15.2 us
  transfers between devices with their start and end apart: 7, of which 7 were waited for; matrix products, arithmetic and copies ran while one was open for 17% of the time, Pallas kernels for 0%

profile of v1, /device:TPU:0, one launch (start us, length us, event | category | flops | bytes accessed | tf_op | source)
XLA Modules:
  0.0 735.2 jit_solution(4334963259660838059)
XLA Ops:
  8.2 1.7 convert_reduce_fusion.1
  9.9 2.1 fusion.24
  13.1 3.3 add_bitcast_fusion
  16.4 3.5 copy.77
  20.0 1.9 slice.129
  22.8 2.6 convolution_convert_fusion
  26.6 1.6 fusion.29
  28.3 32.1 %all_to_all.30 = bf16[16,128,256]{2,1,0:T(8,128)(2,1)} all-to-all(bf16[16,128,256]{2,1,0:T(8,128)(2,1)S(1)} %bitcast.83), channel_id=1, replica_groups=mesh['dp'=2,'seq'=16] {'seq'}, dimensions={0} | all-to-all | bytes 2097152 | tf_op jit(solution)/shard_map/all_to_all | solution.py:196
  60.4 5.2 all-to-all-start
  65.7 31.9 %all-to-all-done.q_ref = bf16[16,192,256]{2,1,0:T(8,128)(2,1)} async-done(((bf16[16,192,256]{2,1,0:T(8,128)(2,1)}), bf16[16,192,256]{2,1,0:T(8,128)(2,1)}, u32[]{:S(2)}, u32[]{:S(2)}) %all-to-all-start) | async-done | bytes 1572896 | tf_op jit(solution)/shard_map/all_to_all | solution.py:196
  97.6 9.2 %all-to-all-start.1 = ((bf16[16,192,256]{2,1,0:T(8,128)(2,1)}), bf16[16,192,256]{2,1,0:T(8,128)(2,1)}, u32[]{:S(2)}, u32[]{:S(2)}) async-start(bf16[16,192,256]{2,1,0:T(8,128)(2,1)} %bitcast.86), calls=%async_computation.1 | async-start | bytes 3145728 | tf_op jit(solution)/shard_map/all_to_all | solution.py:196
  106.8 12.2 %multiply_convert_fusion = (bf16[4,256,3072]{2,1,0:T(8,128)(2,1)}, f32[4,256,3072]{2,1,0:T(8,128)}) fusion(f32[3072]{0:T(1024)S(1)} %copy-done.32, bf16[768,3072]{1,0:T(8,128)(2,1)} %param.33, bf16[4,256,768]{2,1,0:T(8,128)(2,1)S(1)} %copy-done.1, f32[768]{0:T(1024)S(1)} %copy-done.34, f32[768]{0:T(1024)S(1)} %copy-done.21, f32[4,256]{1,0:T(4,128)S(1)} %fusion.63, ...), kind=kOutput, calls=%fused_computation.2 | convolution fusion | flops 4855431168 | bytes 25192448 | tf_op jit(solution)/shard_map/stc,cf->stf/dot_general | solution.py:221
  121.9 2.4 copy.79.k_ref
  124.3 14.5 %all-to-all-done.1.g_ref = bf16[16,192,256]{2,1,0:T(8,128)(2,1)} async-done(((bf16[16,192,256]{2,1,0:T(8,128)(2,1)}), bf16[16,192,256]{2,1,0:T(8,128)(2,1)}, u32[]{:S(2)}, u32[]{:S(2)}) %all-to-all-start.1) | async-done | bytes 1572896 | tf_op jit(solution)/shard_map/all_to_all | solution.py:196
  138.8 142.8 %attention.1 = (bf16[16,192,256]{2,1,0:T(8,128)(2,1)}, bf16[16,192,256]{2,1,0:T(8,128)(2,1)}, f32[4096,64]{1,0:T(8,128)}, f32[4096,64]{1,0:T(8,128)}) custom-call(bf16[16,192,256]{2,1,0:T(8,128)(2,1)} %all-to-all-done.q_ref, bf16[16,192,256]{2,1,0:T(8,128)(2,1)} %all-to-all-done.1.g_ref, bf16[4096,64]{1,0:T(8,128)(2,1)} %copy.79.k_ref, ...), custom_call_target="tpu_custom_call" | custom-call | flops 115964116992 | bytes 3145728 | tf_op jit(solution)/shard_map/attention/pallas_call | solution.py:146
  281.6 1.9 multiply_convert_fusion.1
  284.0 1.6 pad_maximum_fusion.3
  285.5 9.3 %all-to-all-start.5 = ((bf16[16,256,128]{2,1,0:T(8,128)(2,1)}), bf16[16,256,128]{2,1,0:T(8,128)(2,1)}, u32[]{:S(2)}, u32[]{:S(2)}) async-start(bf16[16,256,128]{2,1,0:T(8,128)(2,1)} %pad_maximum_fusion.3), calls=%async_computation.5 | async-start | bytes 2097152 | tf_op jit(solution)/shard_map/all_to_all | solution.py:196
  294.9 15.2 %convert_reduce_fusion = (f32[3072]{0:T(1024)}, bf16[4,256,3072]{2,1,0:T(8,128)(2,1)}) fusion(bf16[4,256,768]{2,1,0:T(8,128)(2,1)} %param.37, bf16[3072,768]{1,0:T(8,128)(2,1)} %param.35, f32[4,256,3072]{2,1,0:T(8,128)} %get-tuple-element.140, f32[3072]{0:T(1024)S(1)} %copy-done.32), kind=kOutput, calls=%fused_computation | convolution fusion | flops 4882166784 | bytes 25190400 | tf_op jit(solution)/shard_map/stc,fc->stf/dot_general | solution.py:227
  310.0 7.8 %all-to-all-done.5 = bf16[16,256,128]{2,1,0:T(8,128)(2,1)} async-done(((bf16[16,256,128]{2,1,0:T(8,128)(2,1)}), bf16[16,256,128]{2,1,0:T(8,128)(2,1)}, u32[]{:S(2)}, u32[]{:S(2)}) %all-to-all-start.5) | async-done | bytes 1048608 | tf_op jit(solution)/shard_map/all_to_all | solution.py:196
  317.8 6.9 all-to-all-start.4
  324.8 10.0 %bitcast_convert_fusion.1 = bf16[768,3072]{1,0:T(8,128)(2,1)} fusion(bf16[4,256,3072]{2,1,0:T(8,128)(2,1)} %get-tuple-element.143, bf16[4,256,768]{2,1,0:T(8,128)(2,1)S(1)} %copy-done.1, f32[768]{0:T(1024)S(1)} %copy-done.34, f32[768]{0:T(1024)S(1)} %copy-done.21, f32[4,256]{1,0:T(4,128)S(1)} %fusion.63, f32[4,256]{1,0:T(4,128)S(1)} %broadcast_multiply_fusion), kind=kOutput, calls=%fused_computation.5 | convolution fusion | flops 4838916096 | bytes 12597248 | tf_op jit(solution)/shard_map/stc,stf->cf/dot_general | solution.py:234
  334.8 9.8 %bitcast_convert_fusion = bf16[3072,768]{1,0:T(8,128)(2,1)} fusion(bf16[4,256,3072]{2,1,0:T(8,128)(2,1)} %get-tuple-element.139, bf16[4,256,768]{2,1,0:T(8,128)(2,1)S(1)} %copy-done.7), kind=kOutput, calls=%fused_computation.4 | convolution fusion | flops 4834197504 | bytes 12582912 | tf_op jit(solution)/shard_map/stf,stc->fc/dot_general | solution.py:231
  344.6 12.6 %all-to-all-done.4 = bf16[16,192,256]{2,1,0:T(8,128)(2,1)} async-done(((bf16[16,192,256]{2,1,0:T(8,128)(2,1)}), bf16[16,192,256]{2,1,0:T(8,128)(2,1)}, u32[]{:S(2)}, u32[]{:S(2)}) %all-to-all-start.4) | async-done | bytes 1572896 | tf_op jit(solution)/shard_map/all_to_all | solution.py:196
  357.2 17.0 %all-to-all-start.3 = ((bf16[16,192,256]{2,1,0:T(8,128)(2,1)}), bf16[16,192,256]{2,1,0:T(8,128)(2,1)}, u32[]{:S(2)}, u32[]{:S(2)}) async-start(bf16[16,192,256]{2,1,0:T(8,128)(2,1)} %get-tuple-element.31), calls=%async_computation.3 | async-start | bytes 3145728 | tf_op jit(solution)/shard_map/all_to_all | solution.py:196
  374.6 10.0 %fusion.9 = f32[4,256,768]{2,1,0:T(8,128)} fusion(bf16[4,256,3072]{2,1,0:T(8,128)(2,1)} %get-tuple-element.143, bf16[768,3072]{1,0:T(8,128)(2,1)} %param.33), kind=kOutput, calls=%fused_computation.20 | convolution fusion | flops 4831838208 | bytes 14155776 | tf_op jit(solution)/shard_map/stf,cf->stc/dot_general | solution.py:235
  386.8 9.7 %fusion.7 = f32[4,256,768]{2,1,0:T(8,128)} fusion(bf16[4,256,3072]{2,1,0:T(8,128)(2,1)} %get-tuple-element.139, bf16[3072,768]{1,0:T(8,128)(2,1)} %param.35), kind=kOutput, calls=%fused_computation.18 | convolution fusion | flops 4831838208 | bytes 14155776 | tf_op jit(solution)/shard_map/stf,fc->stc/dot_general | solution.py:224
  396.6 1.4 bitcast_reduce_fusion
  398.4 1.5 fusion.60
  400.9 1.4 slice.137
  402.3 1.8 convert_element_type.108
  404.3 1.3 pad_maximum_fusion.2
  405.6 2.6 copy.83
  408.2 2.5 convert_reduce_fusion.3
  410.7 10.0 %all-to-all-done.3 = bf16[16,192,256]{2,1,0:T(8,128)(2,1)} async-done(((bf16[16,192,256]{2,1,0:T(8,128)(2,1)}), bf16[16,192,256]{2,1,0:T(8,128)(2,1)}, u32[]{:S(2)}, u32[]{:S(2)}) %all-to-all-start.3) | async-done | bytes 1572896 | tf_op jit(solution)/shard_map/all_to_all | solution.py:196
  420.7 3.4 bitcast_convert_fusion.3
  424.2 2.1 bitcast_convert_fusion.2
  426.3 1.7 pad_maximum_fusion
  428.0 150.3 %all-reduce.6.cloned.1.call-done = (bf16[768,3072]{1,0:T(8,128)(2,1)}, bf16[3072,768]{1,0:T(8,128)(2,1)}) async-done(((bf16[768,3072]{1,0:T(8,128)(2,1)}, bf16[3072,768]{1,0:T(8,128)(2,1)}), (bf16[768,3072]{1,0:T(8,128)(2,1)}, bf16[3072,768]{1,0:T(8,128)(2,1)})) %all-reduce.6.cloned.1.call-update) | async-done | bytes 9437200 | tf_op jit(solution)/shard_map/psum | solution.py:236
  578.3 5.4 fusion.67
  583.8 2.9 fusion.23
  586.8 3.5 convert_reduce_fusion.2
  590.3 40.5 %psum.28 = f32[7808]{0:T(1024)S(1)} all-reduce(f32[7808]{0:T(1024)S(1)} %constant_dynamic-update-slice_fusion), channel_id=1, replica_groups=mesh['dp'=2,'seq'=16] {'dp','seq'}, use_global_device_ids=true, to_apply=%region_14.0 | all-reduce | flops 7808 | bytes 62464 | tf_op jit(solution)/shard_map/psum | solution.py:300
  632.0 7.5 %convert_element_type.119 = f32[768,3072]{1,0:T(8,128)} convert(bf16[768,3072]{1,0:T(8,128)(2,1)} %get-tuple-element.36) | non-fusion elementwise | flops 2359296 | bytes 14155776 | tf_op jit(solution)/shard_map/convert_element_type | solution.py:322
  639.6 4.5 convert_element_type.120
  644.7 4.7 fusion.28
  649.4 71.0 %all-reduce.4.cloned.1.call-done = bf16[768,1664]{1,0:T(8,128)(2,1)} async-done(((bf16[768,1664]{1,0:T(8,128)(2,1)}), bf16[768,1664]{1,0:T(8,128)(2,1)}) %all-reduce.4.cloned.1.call-update) | async-done | bytes 2555920 | tf_op jit(solution)/shard_map/psum | solution.py:300
  723.2 4.2 fusion.68
  (136 shorter events, 17.0 us)
Async XLA Ops:
  7.2 15.6 %copy-start = (bf16[768,768]{1,0:T(8,128)(2,1)S(1)}, bf16[768,768]{1,0:T(8,128)(2,1)}, u32[]{:S(2)}) copy-start(bf16[768,768]{1,0:T(8,128)(2,1)} %param.31) | copy-start | bytes 3538948
  7.2 4.9 copy-start.1
  7.2 4.8 copy-start.37
  7.2 4.8 copy-start.38
  7.2 4.8 copy-start.22
  7.2 4.8 copy-start.35
  7.3 4.8 copy-start.14
  7.3 4.8 copy-start.12
  7.3 14.6 %copy-start.30 = (f32[8]{0:T(128)}, f32[8]{0:T(128)S(1)}, u32[]{:S(2)}) copy-start(f32[8]{0:T(128)S(1)} %multiply_exponential_fusion) | copy-start | bytes 100
  8.2 13.8 %copy-start.18 = (f32[4,256]{1,0:T(4,128)}, f32[4,256]{1,0:T(4,128)S(1)}, u32[]{:S(2)}) copy-start(f32[4,256]{1,0:T(4,128)S(1)} %convert_element_type.98) | copy-start | bytes 12292
  9.9 3.2 copy-start.31
  9.9 3.2 copy-start.33
  20.0 2.8 copy-start.6
  22.8 2.6 copy-start.9
  60.4 46.4 %copy-start.21 = (f32[768]{0:T(1024)S(1)}, f32[768]{0:T(1024)}, u32[]{:S(2)}) copy-start(f32[768]{0:T(1024)} %param.23) | copy-start | bytes 9220
  60.4 46.4 %copy-start.32 = (f32[3072]{0:T(1024)S(1)}, f32[3072]{0:T(1024)}, u32[]{:S(2)}) copy-start(f32[3072]{0:T(1024)} %param.34) | copy-start | bytes 36868
  60.4 46.4 %copy-start.34 = (f32[768]{0:T(1024)S(1)}, f32[768]{0:T(1024)}, u32[]{:S(2)}) copy-start(f32[768]{0:T(1024)} %param.24) | copy-start | bytes 9220
  60.4 37.2 %all-to-all-start = ((bf16[16,192,256]{2,1,0:T(8,128)(2,1)}), bf16[16,192,256]{2,1,0:T(8,128)(2,1)}, u32[]{:S(2)}, u32[]{:S(2)}) async-start(bf16[16,192,256]{2,1,0:T(8,128)(2,1)} %bitcast.77), calls=%async_computation | async-start | bytes 3145728 | tf_op jit(solution)/shard_map/all_to_all | solution.py:196
  97.6 41.2 %all-to-all-start.1 = ((bf16[16,192,256]{2,1,0:T(8,128)(2,1)}), bf16[16,192,256]{2,1,0:T(8,128)(2,1)}, u32[]{:S(2)}, u32[]{:S(2)}) async-start(bf16[16,192,256]{2,1,0:T(8,128)(2,1)} %bitcast.86), calls=%async_computation.1 | async-start | bytes 3145728 | tf_op jit(solution)/shard_map/all_to_all | solution.py:196
  106.8 12.2 %copy-start.4 = (bf16[16,128,256]{2,1,0:T(8,128)(2,1)S(1)}, bf16[16,128,256]{2,1,0:T(8,128)(2,1)}, u32[]{:S(2)}) copy-start(bf16[16,128,256]{2,1,0:T(8,128)(2,1)} %all_to_all.30) | copy-start | bytes 3145732
  281.6 2.2 copy-start.5
  285.5 32.3 %all-to-all-start.5 = ((bf16[16,256,128]{2,1,0:T(8,128)(2,1)}), bf16[16,256,128]{2,1,0:T(8,128)(2,1)}, u32[]{:S(2)}, u32[]{:S(2)}) async-start(bf16[16,256,128]{2,1,0:T(8,128)(2,1)} %pad_maximum_fusion.3), calls=%async_computation.5 | async-start | bytes 2097152 | tf_op jit(solution)/shard_map/all_to_all | solution.py:196
  317.8 39.4 %all-to-all-start.4 = ((bf16[16,192,256]{2,1,0:T(8,128)(2,1)}), bf16[16,192,256]{2,1,0:T(8,128)(2,1)}, u32[]{:S(2)}, u32[]{:S(2)}) async-start(bf16[16,192,256]{2,1,0:T(8,128)(2,1)} %get-tuple-element.32), calls=%async_computation.4 | async-start | bytes 3145728 | tf_op jit(solution)/shard_map/all_to_all | solution.py:196
  324.8 253.5 %all-reduce.6.cloned.1.call-start = ((), (), s32[]{:S(2)}) async-start(), calls=%async_computation.7 | async-start | bytes 18874368 | tf_op jit(solution)/shard_map/psum | solution.py:236
  324.8 10.0 %copy-start.7 = (bf16[4,256,768]{2,1,0:T(8,128)(2,1)S(1)}, bf16[4,256,768]{2,1,0:T(8,128)(2,1)}, u32[]{:S(2)}) copy-start(bf16[4,256,768]{2,1,0:T(8,128)(2,1)} %param.37) | copy-start | bytes 4718596
  357.2 63.5 %all-to-all-start.3 = ((bf16[16,192,256]{2,1,0:T(8,128)(2,1)}), bf16[16,192,256]{2,1,0:T(8,128)(2,1)}, u32[]{:S(2)}, u32[]{:S(2)}) async-start(bf16[16,192,256]{2,1,0:T(8,128)(2,1)} %get-tuple-element.31), calls=%async_computation.3 | async-start | bytes 3145728 | tf_op jit(solution)/shard_map/all_to_all | solution.py:196
  374.3 10.3 %copy-start.13 = (bf16[768,64]{0,1:T(8,128)(2,1)S(1)}, bf16[768,64]{0,1:T(8,128)(2,1)}, u32[]{:S(2)}) copy-start(bf16[768,64]{0,1:T(8,128)(2,1)} %param.27) | copy-start | bytes 294916
  374.3 11.1 %copy-start.15 = (bf16[768,64]{0,1:T(8,128)(2,1)S(1)}, bf16[768,64]{0,1:T(8,128)(2,1)}, u32[]{:S(2)}) copy-start(bf16[768,64]{0,1:T(8,128)(2,1)} %param.29) | copy-start | bytes 294916
  374.3 11.9 %copy-start.27 = (f32[768]{0:T(1024)S(1)}, f32[768]{0:T(1024)}, u32[]{:S(2)}) copy-start(f32[768]{0:T(1024)} %param.32) | copy-start | bytes 9220
  374.3 11.9 %copy-start.28 = (f32[768]{0:T(1024)S(1)}, f32[768]{0:T(1024)}, u32[]{:S(2)}) copy-start(f32[768]{0:T(1024)} %param.36) | copy-start | bytes 9220
  374.3 346.0 %all-reduce.4.cloned.1.call-start = ((), (), s32[]{:S(2)}) async-start(), calls=%async_computation.6 | async-start | bytes 5111808 | tf_op jit(solution)/shard_map/psum | solution.py:300
  396.6 1.8 copy-start.19
  400.9 3.2 copy-start.10
  400.9 3.2 copy-start.11
  420.7 3.4 copy-start.3
  420.7 3.4 copy-start.23
  420.7 3.4 copy-start.36
  578.3 5.4 copy-start.17
  578.3 5.4 copy-start.2
  583.7 2.9 copy-start.20
  583.8 2.9 copy-start.24
  583.8 3.0 copy-start.8
  586.7 3.6 copy-start.26
  586.8 52.8 %slice-start = ((s8[4718592]{0:T(1024)(128)(4,1)}), s8[524288]{0:T(1024)(128)(4,1)S(1)}, s32[]{:S(2)}) async-start(s8[4718592]{0:T(1024)(128)(4,1)} %bitcast.78), calls=%async_computation.8 | async-start | bytes 1048576
  632.0 95.3 %copy-start.25 = (f32[768]{0:T(1024)}, f32[768]{0:T(1024)S(1)}, u32[]{:S(2)}) copy-start(f32[768]{0:T(1024)S(1)} %get-tuple-element.181) | copy-start | bytes 9220
  632.0 7.5 %slice-start.1 = ((s8[4718592]{0:T(1024)(128)(4,1)}), s8[4194304]{0:T(1024)(128)(4,1)S(1)}, s32[]{:S(2)}) async-start(s8[4718592]{0:T(1024)(128)(4,1)} %bitcast.78), calls=%async_computation.9 | async-start | bytes 8388608
  639.6 5.1 copy-start.29
  639.6 5.1 copy-start.39
  (1 other events, 1.1 us)
Sparse Core Ops, SparseCore 0:
  344.7 233.5 all-reduce.5
  584.6 135.7 all-reduce.3

commit v2 on v1

--- a/solution.py
+++ b/solution.py
@@ -1,3 +1,4 @@
+import functools
 import math
 
 import jax
@@ -152,10 +153,115 @@
         scratch_shapes=[pltpu.VMEM((length, lanes), F32), pltpu.VMEM((length, lanes), BF)],
         compiler_params=pltpu.CompilerParams(vmem_limit_bytes=56 * 2**20),
         cost_estimate=pl.CostEstimate(
-            flops=6 * flops, bytes_accessed=4 * q.size, transcendentals=length * length // 2 * 3
+            flops=flops, bytes_accessed=4 * q.size, transcendentals=length * length // 2 * 3
         ),
         name="attention",
     )(q, g, key, jnp.concatenate([value, ones], axis=1), key.T, value.T)
+
+
+MESH=pl.DeviceIdType.MESH
+
+def bit_orders(dp, ring):
+    seq_bits = [("seq", 1 << b) for b in range(ring.bit_length() - 1)]
+    dp_bits = [("dp", 1 << b) for b in range(dp.bit_length() - 1)]
+    far = seq_bits[2:]
+    return (seq_bits[:2] + dp_bits + far, seq_bits[:1] + dp_bits + seq_bits[1:2] + far)
+
+def side_of(bit):
+    axis, weight = bit
+    return lax.rem(lax.axis_index(axis) // weight, 2)
+
+def partner_of(bit):
+    axis, weight = bit
+    me = lax.axis_index(axis)
+    return {axis: me + weight - 2 * weight * side_of(bit)}
+
+def add_rows(dst, a, b, dst_at, a_at, rows, step):
+    def body(i, carry):
+        r = pl.multiple_of(i * step, step)
+        dst[pl.ds(dst_at + r, step), :] = a[pl.ds(a_at + r, step), :] + b[pl.ds(r, step), :]
+        return carry
+    lax.fori_loop(0, rows // step, body, 0)
+
+def sum_kernel(orders, x_ref, out_ref, *scratch):
+    parts = len(orders)
+    stages = len(orders[0])
+    rows, cols = x_ref.shape
+    wide = cols // parts
+    acc, recv, sems = scratch[:parts], scratch[parts:2*parts], scratch[2*parts:]
+    send_sem, recv_sem = sems
+    barrier = pltpu.get_barrier_semaphore()
+    for bit in orders[0]:
+        pl.semaphore_signal(barrier, inc=1, device_id=partner_of(bit), device_id_type=MESH)
+    pl.semaphore_wait(barrier, stages)
+    def copy(p, s, src, dst, bit):
+        return pltpu.make_async_remote_copy(src_ref=src, dst_ref=dst, send_sem=send_sem.at[p, s], recv_sem=recv_sem.at[p, s],
+            device_id=partner_of(bit), device_id_type=MESH)
+    columns = [pl.ds(p * wide, wide) for p in range(parts)]
+    start = [0] * parts
+    whole = [0] * parts
+    live = {}
+    base = [0]
+    for s in range(stages): base.append(base[-1] + rows // 2 ** min(s + 1, stages - 1))
+    def launch(p, s):
+        bit = orders[p][s]
+        if s < stages - 1:
+            half = rows // 2 ** (s + 1)
+            other = pl.multiple_of(start[p] + (1 - side_of(bit)) * half, half)
+            src = x_ref.at[pl.ds(other, half), columns[p]] if s == 0 else acc[p].at[pl.ds(other, half), :]
+        else:
+            half = rows // 2 ** s
+            src = acc[p].at[pl.ds(pl.multiple_of(start[p], half), half), :]
+        live[p] = copy(p, s, src, recv[p].at[pl.ds(base[s], half), :], bit)
+        live[p].start()
+    for p in range(parts): launch(p, 0)
+    for s in range(stages):
+        for p in range(parts):
+            bit = orders[p][s]
+            live[p].wait()
+            half = rows // 2 ** min(s + 1, stages - 1)
+            step = 16 if half % 64 else 64
+            got = recv[p].at[pl.ds(base[s], half), :]
+            if s == 0:
+                mine = side_of(bit) * half
+                whole[p] = mine
+                add_rows(acc[p], x_ref.at[:, columns[p]], got, 0, pl.multiple_of(mine, half), half, step)
+                start[p] = 0
+            elif s < stages - 1:
+                mine = pl.multiple_of(start[p] + side_of(bit) * half, half)
+                add_rows(acc[p], acc[p], got, mine, mine, half, step)
+                whole[p] = whole[p] + side_of(bit) * half
+                start[p] = start[p] + side_of(bit) * half
+            else:
+                at = pl.multiple_of(start[p], half)
+                add_rows(out_ref.at[:, columns[p]], acc[p], got, pl.multiple_of(whole[p], half), at, half, step)
+            if s < stages - 1: launch(p, s + 1)
+    def spread(p, s):
+        bit = orders[p][s]
+        half = rows // 2 ** (s + 1)
+        src = out_ref.at[pl.ds(pl.multiple_of(whole[p], half), half), columns[p]]
+        live[p] = copy(p, 2 * stages - 2 - s, src, src, bit)
+        live[p].start()
+    for p in range(parts): spread(p, stages - 2)
+    for s in range(stages - 2, -1, -1):
+        for p in range(parts):
+            live[p].wait()
+            whole[p] = whole[p] - side_of(orders[p][s]) * (rows // 2 ** (s + 1))
+            if s: spread(p, s - 1)
+
+def total_of(x, dp, ring, collective_id):
+    orders = bit_orders(dp, ring)
+    rows, cols = x.shape
+    parts, stages = len(orders), len(orders[0])
+    wide = cols // parts
+    got = sum(rows // 2 ** min(s + 1, stages - 1) for s in range(stages))
+    whole = pl.BlockSpec(memory_space=pltpu.VMEM)
+    return pl.pallas_call(functools.partial(sum_kernel, orders),
+        out_shape=jax.ShapeDtypeStruct(x.shape, BF), in_specs=[whole], out_specs=whole,
+        scratch_shapes=[pltpu.VMEM((rows // 2, wide), BF)] * parts + [pltpu.VMEM((got, wide), BF)] * parts
+        + [pltpu.SemaphoreType.DMA((parts, 2 * stages - 1))] * 2,
+        compiler_params=pltpu.CompilerParams(collective_id=collective_id, has_side_effects=True, vmem_limit_bytes=56*2**20),
+        name="total")(x)
 
 
 def local(
@@ -233,7 +339,10 @@
     ).astype(BF)
     grad_w_up = jnp.einsum("stc,stf->cf", normed_m, grad_up, preferred_element_type=F32).astype(BF)
     grad_normed_m = jnp.einsum("stf,cf->stc", grad_up, up_weight, preferred_element_type=F32)
-    grad_w_up, grad_w_down = lax.psum((grad_w_up, grad_w_down), ("dp", "seq"))
+    kv_here, query_here, grad_here, grad_w_up, grad_w_down, feedforward, grad_normed_m = lax.optimization_barrier(
+        (kv_here, query_here, grad_here, grad_w_up, grad_w_down, feedforward, grad_normed_m)
+    )
+    grad_w_down = lax.psum(grad_w_down, ("dp", "seq"))
     grad_b_up = jnp.sum(grad_up.astype(F32), axis=(0, 1))
     grad_b_down = jnp.sum(cotangent.astype(F32), axis=(0, 1))
 
@@ -251,6 +360,10 @@
     out, dq, dk, dv = attention(
         to_tiles(query_here), to_tiles(grad_here), kv_rows[:, :HEAD_DIM], kv_rows[:, HEAD_DIM:]
     )
+    out, dq, dk, dv, grad_w_up, grad_w_down = lax.optimization_barrier(
+        (out, dq, dk, dv, grad_w_up, grad_w_down)
+    )
+    grad_w_up = lax.psum(grad_w_up, ("dp", "seq"))
     attended = swap(from_tiles(out)).reshape(seq_count, D, local_len)
     query_back = swap(from_tiles(dq)).reshape(seq_count, HEADS, HEAD_DIM, local_len)
     kv_part = jnp.concatenate([dk * (1.0 / LOG2E), dv], axis=1).astype(BF)
@@ -292,18 +405,30 @@
             grad_b_down,
         ]
     )
+    dp = lax.axis_size("dp")
+    unit = 16 * dp * ring // 2
+    square = D * (2 * D + 2 * HEAD_DIM)
+    filled = square // D + -(-vectors.size // D)
+    padded = -(-filled // unit) * unit
     rest = jnp.concatenate(
-        [grad_w_qkv, grad_w_out],
-        axis=1,
+        [
+            grad_w_qkv[:, :D],
+            grad_w_out,
+            grad_w_qkv[:, D:].T,
+            jnp.pad(vectors, (0, (padded * D - square) - vectors.size)).reshape(-1, D),
+        ],
+        axis=0,
     ).astype(BF)
-    rest, grad_w_up, grad_w_down = lax.optimization_barrier((rest, grad_w_up, grad_w_down))
-    rest, vectors = lax.psum((rest, vectors), ("dp", "seq"))
+    rest = total_of(rest, dp, ring, 3)
+    rest, grad_w_up = lax.optimization_barrier((rest, grad_w_up))
     rest = rest.astype(F32)
+    vectors = rest[square // D :].reshape(-1)
+    rest_kv = rest[2 * D : 2 * D + 2 * HEAD_DIM]
     qkv = D + 2 * HEAD_DIM
     ff = up_weight.shape[1]
     b_qkv = vectors[4 * D : 4 * D + qkv]
     b_up = vectors[4 * D + qkv : 4 * D + qkv + ff]
-    b_down = vectors[4 * D + qkv + ff :]
+    b_down = vectors[4 * D + qkv + ff : 4 * D + qkv + ff + D]
     return (
         layer_out,
         input_grad,
@@ -311,13 +436,13 @@
         vectors[D : 2 * D],
         vectors[2 * D : 3 * D],
         vectors[3 * D : 4 * D],
-        rest[:, :D],
+        rest[:D],
         b_qkv[:D],
-        rest[:, D : D + HEAD_DIM],
+        rest_kv[:HEAD_DIM].T,
         b_qkv[D : D + HEAD_DIM],
-        rest[:, D + HEAD_DIM : qkv],
+        rest_kv[HEAD_DIM:].T,
         b_qkv[D + HEAD_DIM :],
-        rest[:, qkv:],
+        rest[D : 2 * D],
         b_down,
         grad_w_up.astype(F32),
         b_up,

time: 744 us -> 570 us (0.77)
  waiting for transfers between devices: 298 us -> 89.4 us
  Pallas kernels: 143 us -> 205 us
  blocking collectives: 72.6 us -> 30 us
  local copies, waits for them, and re-layouts: 27.7 us -> 44.2 us
    psum x2, waiting for transfers between devices: 221 us -> 35.4 us  [the longest x1 31.4 us: local(): grad_w_up = lax.psum(grad_w_up, ('dp', 'seq'))]
    pallas_call x0 -> x1, Pallas kernels: none -> 62.3 us  [total_of(): pl.pallas_call(functools.partial(sum_kernel, orders), out_shape=jax.Shape...]
    psum x1 -> x0, blocking collectives: 40.5 us -> none  [local(): rest, vectors = lax.psum((rest, vectors), ('dp', 'seq'))]
    all_to_all x5, waiting for transfers between devices: 76.9 us -> 53.9 us  [swap(): return lax.all_to_all(x, 'seq', split_axis=0, concat_axis=0, tiled=True)]
    unnamed x95 -> x109, local copies, waits for them, and re-layouts: 4.44 us -> 12.8 us
  transfers between devices with their start and end apart: 7 -> 7, of which waited for: 7 -> 5; matrix products, arithmetic and copies ran while one was open for 17% -> 22% of each run, Pallas kernels for 0% -> 36%
where the time goes in v2:
time: 570 us; the launch traced here: 567 us
  Pallas kernels  205 us (36%)
  waiting for transfers between devices  89.4 us (16%)
  matrix products  86.4 us (15%)
  starting transfers between devices  49.7 us (9%)
  other arithmetic  46.8 us (8%)
  local copies, waits for them, and re-layouts  44.2 us (8%)
  blocking collectives  30 us (5%)
  between operations  15.2 us (3%)
    pallas_call x1, Pallas kernels, attention(): pl.pallas_call(attention_kernel, out_shape=[jax.ShapeDtypeStruct(q.shape,...  143 us
    pallas_call x1, Pallas kernels, total_of(): pl.pallas_call(functools.partial(sum_kernel, orders), out_shape=jax.Shape...  62.3 us
    all_to_all x5, waiting for transfers between devices, swap(): return lax.all_to_all(x, 'seq', split_axis=0, concat_axis=0, tiled=True)  53.9 us
    all_to_all x5, starting transfers between devices, swap(): return lax.all_to_all(x, 'seq', split_axis=0, concat_axis=0, tiled=True)  49.6 us
    psum x1, waiting for transfers between devices, local(): grad_w_up = lax.psum(grad_w_up, ('dp', 'seq'))  31.4 us
    all_to_all x1, blocking collectives, swap(): return lax.all_to_all(x, 'seq', split_axis=0, concat_axis=0, tiled=True)  30 us
    dot_general x1, matrix products, local(): jnp.einsum('stc,fc->stf', cotangent, down_weight, preferred_element_type=...  13.9 us
    unnamed x109, local copies, waits for them, and re-layouts  12.8 us
  transfers between devices with their start and end apart: 7, of which 5 were waited for; matrix products, arithmetic and copies ran while one was open for 22% of the time, Pallas kernels for 36%

profile of v2, /device:TPU:0, one launch (start us, length us, event | category | flops | bytes accessed | tf_op | source)
XLA Modules:
  0.0 566.8 jit_solution(13040268576272611415)
XLA Ops:
  7.3 1.8 convert_reduce_fusion
  9.1 2.0 fusion.23
  11.2 3.3 add_bitcast_fusion
  14.5 3.5 copy.73
  18.1 1.9 slice.171
  23.2 2.6 convolution_convert_fusion
  25.8 1.6 fusion.28
  28.4 7.5 %all-to-all-start = ((bf16[16,128,256]{2,1,0:T(8,128)(2,1)}), bf16[16,128,256]{2,1,0:T(8,128)(2,1)}, u32[]{:S(2)}, u32[]{:S(2)}) async-start(bf16[16,128,256]{2,1,0:T(8,128)(2,1)} %bitcast.87), calls=%async_computation | async-start | bytes 2097152 | tf_op jit(solution)/shard_map/all_to_all | solution.py:302
  36.2 10.9 %multiply_convert_fusion = (bf16[4,256,3072]{2,1,0:T(8,128)(2,1)}, f32[4,256,3072]{2,1,0:T(8,128)S(1)}) fusion(f32[3072]{0:T(1024)S(1)} %copy-done.40, bf16[768,3072]{1,0:T(8,128)(2,1)} %param.33, bf16[4,256,768]{2,1,0:T(8,128)(2,1)S(1)} %copy-done.2, f32[768]{0:T(1024)S(1)} %copy-done.42, f32[768]{0:T(1024)S(1)} %copy-done.24, f32[4,256]{1,0:T(4,128)S(1)} %fusion.62, ...), kind=kOutput, calls=%fused_computation | convolution fusion | flops 4855431168 | bytes 25192448 | tf_op jit(solution)/shard_map/stc,cf->stf/dot_general | solution.py:327
  47.1 13.9 %fusion.70 = (bf16[3072]{0:T(1024)(128)(2,1)}, bf16[4,256,3072]{2,1,0:T(8,128)(2,1)}) fusion(bf16[4,256,768]{2,1,0:T(8,128)(2,1)S(1)} %copy-done.8, bf16[3072,768]{1,0:T(8,128)(2,1)S(1)} %bitcast.91, f32[4,256,3072]{2,1,0:T(8,128)S(1)} %get-tuple-element.105, f32[3072]{0:T(1024)S(1)} %copy-done.40), kind=kOutput, calls=%fused_computation.119 | convolution fusion | flops 4879021056 | bytes 25184256 | tf_op jit(solution)/shard_map/stc,fc->stf/dot_general | solution.py:333
  60.9 16.3 %all-to-all-start.1 = ((bf16[16,192,256]{2,1,0:T(8,128)(2,1)}), bf16[16,192,256]{2,1,0:T(8,128)(2,1)}, u32[]{:S(2)}, u32[]{:S(2)}) async-start(bf16[16,192,256]{2,1,0:T(8,128)(2,1)} %bitcast.83), calls=%async_computation.1 | async-start | bytes 3145728 | tf_op jit(solution)/shard_map/all_to_all | solution.py:302
  77.3 10.0 %fusion.9 = f32[4,256,768]{2,1,0:T(8,128)} fusion(bf16[4,256,3072]{2,1,0:T(8,128)(2,1)} %get-tuple-element.108, bf16[768,3072]{1,0:T(8,128)(2,1)} %param.33), kind=kOutput, calls=%fused_computation.19 | convolution fusion | flops 4831838208 | bytes 14155776 | tf_op jit(solution)/shard_map/stf,cf->stc/dot_general | solution.py:341
  87.2 7.6 %bitcast_convert_fusion.1 = bf16[768,3072]{1,0:T(8,128)(2,1)} fusion(bf16[4,256,3072]{2,1,0:T(8,128)(2,1)S(1)} %copy-done.47, bf16[4,256,768]{2,1,0:T(8,128)(2,1)S(1)} %copy-done.2, f32[768]{0:T(1024)S(1)} %copy-done.42, f32[768]{0:T(1024)S(1)} %copy-done.24, f32[4,256]{1,0:T(4,128)S(1)} %fusion.62, f32[4,256]{1,0:T(4,128)S(1)} %broadcast_multiply_fusion), kind=kOutput, calls=%fused_computation.4 | convolution fusion | flops 4838916096 | bytes 12597248 | tf_op jit(solution)/shard_map/stc,stf->cf/dot_general | solution.py:340
  94.8 14.5 %all-to-all-done.1.q_ref = bf16[16,192,256]{2,1,0:T(8,128)(2,1)} async-done(((bf16[16,192,256]{2,1,0:T(8,128)(2,1)}), bf16[16,192,256]{2,1,0:T(8,128)(2,1)}, u32[]{:S(2)}, u32[]{:S(2)}) %all-to-all-start.1) | async-done | bytes 1572896 | tf_op jit(solution)/shard_map/all_to_all | solution.py:302
  109.3 9.1 %all-to-all-start.2 = ((bf16[16,192,256]{2,1,0:T(8,128)(2,1)}), bf16[16,192,256]{2,1,0:T(8,128)(2,1)}, u32[]{:S(2)}, u32[]{:S(2)}) async-start(bf16[16,192,256]{2,1,0:T(8,128)(2,1)} %bitcast.89), calls=%async_computation.2 | async-start | bytes 3145728 | tf_op jit(solution)/shard_map/all_to_all | solution.py:302
  118.5 9.8 %fusion.6 = f32[4,256,768]{2,1,0:T(8,128)} fusion(bf16[4,256,3072]{2,1,0:T(8,128)(2,1)} %get-tuple-element.104, bf16[3072,768]{1,0:T(8,128)(2,1)} %param.35), kind=kOutput, calls=%fused_computation.16 | convolution fusion | flops 4831838208 | bytes 14155776 | tf_op jit(solution)/shard_map/stf,fc->stc/dot_general | solution.py:330
  128.3 9.7 %bitcast_convert_fusion = bf16[3072,768]{1,0:T(8,128)(2,1)} fusion(bf16[4,256,3072]{2,1,0:T(8,128)(2,1)} %get-tuple-element.104, bf16[4,256,768]{2,1,0:T(8,128)(2,1)S(1)} %copy-done.9), kind=kOutput, calls=%fused_computation.3 | convolution fusion | flops 4834197504 | bytes 12582912 | tf_op jit(solution)/shard_map/stf,stc->fc/dot_general | solution.py:337
  138.0 12.5 %all-to-all-done.2.g_ref = bf16[16,192,256]{2,1,0:T(8,128)(2,1)} async-done(((bf16[16,192,256]{2,1,0:T(8,128)(2,1)}), bf16[16,192,256]{2,1,0:T(8,128)(2,1)}, u32[]{:S(2)}, u32[]{:S(2)}) %all-to-all-start.2) | async-done | bytes 1572896 | tf_op jit(solution)/shard_map/all_to_all | solution.py:302
  156.9 142.9 %attention.1 = (bf16[16,192,256]{2,1,0:T(8,128)(2,1)}, bf16[16,192,256]{2,1,0:T(8,128)(2,1)}, f32[4096,64]{1,0:T(8,128)}, f32[4096,64]{1,0:T(8,128)}) custom-call(bf16[16,192,256]{2,1,0:T(8,128)(2,1)} %all-to-all-done.1.q_ref, bf16[16,192,256]{2,1,0:T(8,128)(2,1)} %all-to-all-done.2.g_ref, bf16[4096,64]{1,0:T(8,128)(2,1)} %copy.77.k_ref, ...), custom_call_target="tpu_custom_call" | custom-call | flops 19327352832 | bytes 3145728 | tf_op jit(solution)/shard_map/attention/pallas_call | solution.py:147
  299.8 4.0 all-reduce.4.cloned.1.call-done
  303.8 1.8 convert.78
  306.8 30.0 %all_to_all.30 = bf16[16,256,128]{2,1,0:T(8,128)(2,1)} all-to-all(bf16[16,256,128]{2,1,0:T(8,128)(2,1)S(1)} %pad_maximum_fusion.3), channel_id=1, replica_groups=mesh['dp'=2,'seq'=16] {'seq'}, dimensions={0} | all-to-all | bytes 2097152 | tf_op jit(solution)/shard_map/all_to_all | solution.py:302
  336.8 5.2 all-to-all-start.4
  343.7 2.3 reduce.3
  346.6 6.9 %convert_element_type.122 = f32[3072,768]{1,0:T(8,128)} convert(bf16[3072,768]{1,0:T(8,128)(2,1)} %all-reduce.4.cloned.1.call-done) | non-fusion elementwise | flops 2359296 | bytes 14155776 | tf_op jit(solution)/shard_map/convert_element_type | solution.py:449
  354.0 1.5 fusion.59
  356.6 27.0 %all-to-all-done.4 = bf16[16,192,256]{2,1,0:T(8,128)(2,1)} async-done(((bf16[16,192,256]{2,1,0:T(8,128)(2,1)}), bf16[16,192,256]{2,1,0:T(8,128)(2,1)}, u32[]{:S(2)}, u32[]{:S(2)}) %all-to-all-start.4) | async-done | bytes 1572896 | tf_op jit(solution)/shard_map/all_to_all | solution.py:302
  383.6 11.4 %all-to-all-start.3 = ((bf16[16,192,256]{2,1,0:T(8,128)(2,1)}), bf16[16,192,256]{2,1,0:T(8,128)(2,1)}, u32[]{:S(2)}, u32[]{:S(2)}) async-start(bf16[16,192,256]{2,1,0:T(8,128)(2,1)} %get-tuple-element.52), calls=%async_computation.3 | async-start | bytes 3145728 | tf_op jit(solution)/shard_map/all_to_all | solution.py:302
  396.4 1.8 convert_element_type.113
  399.7 2.6 copy.81
  402.4 6.0 %fusion.67 = (bf16[768]{0:T(1024)(128)(2,1)}, f32[4,256]{1,0:T(4,128)S(1)}, f32[4,256]{1,0:T(4,128)S(1)}, bf16[768]{0:T(1024)(128)(2,1)}, f32[4,256,768]{2,1,0:T(8,128)S(1)}) fusion(f32[768]{0:T(1024)S(1)} %copy-done.28, f32[4,256]{1,0:T(4,128)S(1)} %broadcast_multiply_fusion, bf16[4,256,768]{2,1,0:T(8,128)(2,1)S(1)} %copy-done.2, ...), kind=kOutput, calls=%fused_computation.116 | convolution fusion | flops 1428615680 | bytes 11097088 | tf_op jit(solution)/shard_map/swt,cw->stc/dot_general | solution.py:392
  408.4 3.2 fusion.22
  411.6 1.4 dynamic-update-slice
  415.9 1.4 dynamic-update-slice.3
  417.4 2.5 fusion.65
  421.3 1.5 dynamic-update-slice.5
  425.6 1.8 reshape.180
  427.4 3.5 bitcast_convert_fusion.2
  433.1 2.4 copy.90
  436.4 3.4 bitcast_convert_fusion.3
  439.8 1.7 pad_maximum_fusion.x_ref
  441.5 62.3 %total.1 = bf16[1792,768]{1,0:T(8,128)(2,1)} custom-call(bf16[1792,768]{1,0:T(8,128)(2,1)} %pad_maximum_fusion.x_ref), custom_call_target="tpu_custom_call" | custom-call | tf_op jit(solution)/shard_map/total/pallas_call | solution.py:259
  503.8 31.4 %all-reduce.6.cloned.1.call-done = bf16[768,3072]{1,0:T(8,128)(2,1)} async-done(((bf16[768,3072]{1,0:T(8,128)(2,1)}), bf16[768,3072]{1,0:T(8,128)(2,1)}) %all-reduce.6.cloned.1.call-update) | async-done | bytes 4718608 | tf_op jit(solution)/shard_map/psum | solution.py:366
  535.2 2.3 convert_element_type.120
  537.8 2.5 fusion.68
  543.0 7.5 %convert_element_type.121 = f32[768,3072]{1,0:T(8,128)} convert(bf16[768,3072]{1,0:T(8,128)(2,1)} %all-reduce.6.cloned.1.call-done) | non-fusion elementwise | flops 2359296 | bytes 14155776 | tf_op jit(solution)/shard_map/convert_element_type | solution.py:447
  550.6 4.8 fusion.27
  555.5 3.4 add_add_fusion.2
  (160 shorter events, 32.6 us)
Async XLA Ops:
  7.2 16.0 %copy-start = (bf16[768,768]{1,0:T(8,128)(2,1)S(1)}, bf16[768,768]{1,0:T(8,128)(2,1)}, u32[]{:S(2)}) copy-start(bf16[768,768]{1,0:T(8,128)(2,1)} %param.31) | copy-start | bytes 3538948
  7.2 3.9 copy-start.2
  7.2 3.9 copy-start.41
  7.2 3.9 copy-start.39
  7.2 3.9 copy-start.43
  7.3 3.9 copy-start.27
  7.3 13.9 %copy-start.38 = (f32[8]{0:T(128)}, f32[8]{0:T(128)S(1)}, u32[]{:S(2)}) copy-start(f32[8]{0:T(128)S(1)} %multiply_exponential_fusion) | copy-start | bytes 100
  11.1 3.4 copy-start.22
  21.9 3.8 copy-start.16
  27.3 8.8 %copy-start.24 = (f32[768]{0:T(1024)S(1)}, f32[768]{0:T(1024)}, u32[]{:S(2)}) copy-start(f32[768]{0:T(1024)} %param.23) | copy-start | bytes 9220
  27.3 8.8 %copy-start.40 = (f32[3072]{0:T(1024)S(1)}, f32[3072]{0:T(1024)}, u32[]{:S(2)}) copy-start(f32[3072]{0:T(1024)} %param.34) | copy-start | bytes 36868
  27.3 8.8 %copy-start.42 = (f32[768]{0:T(1024)S(1)}, f32[768]{0:T(1024)}, u32[]{:S(2)}) copy-start(f32[768]{0:T(1024)} %param.24) | copy-start | bytes 9220
  28.4 18.6 %slice-start = ((s8[4718592]{0:T(1024)(128)(4,1)}), s8[524288]{0:T(1024)(128)(4,1)S(1)}, s32[]{:S(2)}) async-start(s8[4718592]{0:T(1024)(128)(4,1)} %bitcast.90), calls=%async_computation.8 | async-start | bytes 1048576
  28.4 32.5 %all-to-all-start = ((bf16[16,128,256]{2,1,0:T(8,128)(2,1)}), bf16[16,128,256]{2,1,0:T(8,128)(2,1)}, u32[]{:S(2)}, u32[]{:S(2)}) async-start(bf16[16,128,256]{2,1,0:T(8,128)(2,1)} %bitcast.87), calls=%async_computation | async-start | bytes 2097152 | tf_op jit(solution)/shard_map/all_to_all | solution.py:302
  36.2 10.9 %copy-start.8 = (bf16[4,256,768]{2,1,0:T(8,128)(2,1)S(1)}, bf16[4,256,768]{2,1,0:T(8,128)(2,1)}, u32[]{:S(2)}) copy-start(bf16[4,256,768]{2,1,0:T(8,128)(2,1)} %param.37) | copy-start | bytes 4718596
  36.2 10.9 %slice-start.1 = ((s8[4718592]{0:T(1024)(128)(4,1)}), s8[4194304]{0:T(1024)(128)(4,1)S(1)}, s32[]{:S(2)}) async-start(s8[4718592]{0:T(1024)(128)(4,1)} %bitcast.90), calls=%async_computation.9 | async-start | bytes 8388608
  60.9 48.3 %all-to-all-start.1 = ((bf16[16,192,256]{2,1,0:T(8,128)(2,1)}), bf16[16,192,256]{2,1,0:T(8,128)(2,1)}, u32[]{:S(2)}, u32[]{:S(2)}) async-start(bf16[16,192,256]{2,1,0:T(8,128)(2,1)} %bitcast.83), calls=%async_computation.1 | async-start | bytes 3145728 | tf_op jit(solution)/shard_map/all_to_all | solution.py:302
  77.3 10.0 %copy-start.47 = (bf16[4,256,3072]{2,1,0:T(8,128)(2,1)S(1)}, bf16[4,256,3072]{2,1,0:T(8,128)(2,1)}, u32[]{:S(2)}) copy-start(bf16[4,256,3072]{2,1,0:T(8,128)(2,1)} %get-tuple-element.108) | copy-start | bytes 18874372
  109.3 41.2 %all-to-all-start.2 = ((bf16[16,192,256]{2,1,0:T(8,128)(2,1)}), bf16[16,192,256]{2,1,0:T(8,128)(2,1)}, u32[]{:S(2)}, u32[]{:S(2)}) async-start(bf16[16,192,256]{2,1,0:T(8,128)(2,1)} %bitcast.89), calls=%async_computation.2 | async-start | bytes 3145728 | tf_op jit(solution)/shard_map/all_to_all | solution.py:302
  118.4 185.4 %all-reduce.4.cloned.1.call-start = ((), (), s32[]{:S(2)}) async-start(), calls=%async_computation.6 | async-start | bytes 9437184 | tf_op jit(solution)/shard_map/psum | solution.py:345
  118.5 9.8 %copy-start.9 = (bf16[4,256,768]{2,1,0:T(8,128)(2,1)S(1)}, bf16[4,256,768]{2,1,0:T(8,128)(2,1)}, u32[]{:S(2)}) copy-start(bf16[4,256,768]{2,1,0:T(8,128)(2,1)} %param.37) | copy-start | bytes 4718596
  306.8 36.0 %copy-start.21 = (bf16[768,64]{0,1:T(8,128)(2,1)S(1)}, bf16[768,64]{0,1:T(8,128)(2,1)}, u32[]{:S(2)}) copy-start(bf16[768,64]{0,1:T(8,128)(2,1)} %param.27) | copy-start | bytes 294916
  336.8 9.1 %copy-start.34 = (f32[768]{0:T(1024)S(1)}, f32[768]{0:T(1024)}, u32[]{:S(2)}) copy-start(f32[768]{0:T(1024)} %param.32) | copy-start | bytes 9220
  336.8 9.1 %copy-start.35 = (f32[768]{0:T(1024)S(1)}, f32[768]{0:T(1024)}, u32[]{:S(2)}) copy-start(f32[768]{0:T(1024)} %param.36) | copy-start | bytes 9220
  336.8 46.8 %all-to-all-start.4 = ((bf16[16,192,256]{2,1,0:T(8,128)(2,1)}), bf16[16,192,256]{2,1,0:T(8,128)(2,1)}, u32[]{:S(2)}, u32[]{:S(2)}) async-start(bf16[16,192,256]{2,1,0:T(8,128)(2,1)} %get-tuple-element.54), calls=%async_computation.4 | async-start | bytes 3145728 | tf_op jit(solution)/shard_map/all_to_all | solution.py:302
  342.0 193.2 %all-reduce.6.cloned.1.call-start = ((), (), s32[]{:S(2)}) async-start(), calls=%async_computation.7 | async-start | bytes 9437184 | tf_op jit(solution)/shard_map/psum | solution.py:366
  346.6 6.9 %copy-start.12 = (bf16[16,256,128]{2,1,0:T(8,128)(2,1)S(1)}, bf16[16,256,128]{2,1,0:T(8,128)(2,1)}, u32[]{:S(2)}) copy-start(bf16[16,256,128]{2,1,0:T(8,128)(2,1)} %all_to_all.30) | copy-start | bytes 3145732
  383.6 52.8 %all-to-all-start.3 = ((bf16[16,192,256]{2,1,0:T(8,128)(2,1)}), bf16[16,192,256]{2,1,0:T(8,128)(2,1)}, u32[]{:S(2)}, u32[]{:S(2)}) async-start(bf16[16,192,256]{2,1,0:T(8,128)(2,1)} %get-tuple-element.52), calls=%async_computation.3 | async-start | bytes 3145728 | tf_op jit(solution)/shard_map/all_to_all | solution.py:302
  395.0 3.2 copy-start.17
  395.0 3.2 copy-start.18
  398.4 3.9 copy-start.28
  402.3 6.1 %copy-start.23 = (f32[4,256]{1,0:T(4,128)S(1)}, f32[4,256]{1,0:T(4,128)}, u32[]{:S(2)}) copy-start(f32[4,256]{1,0:T(4,128)} %copy-done.22) | copy-start | bytes 12292
  402.3 6.1 %copy-start.3 = (f32[4,256,768]{2,1,0:T(8,128)S(1)}, f32[4,256,768]{2,1,0:T(8,128)}, u32[]{:S(2)}) copy-start(f32[4,256,768]{2,1,0:T(8,128)} %fusion.9) | copy-start | bytes 9437188
  402.3 6.1 %copy-start.25 = (f32[768]{0:T(1024)S(1)}, f32[768]{0:T(1024)}, u32[]{:S(2)}) copy-start(f32[768]{0:T(1024)} %param.23) | copy-start | bytes 9220
  402.3 6.1 %copy-start.29 = (f32[768]{0:T(1024)S(1)}, f32[768]{0:T(1024)}, u32[]{:S(2)}) copy-start(f32[768]{0:T(1024)} %param.21) | copy-start | bytes 9220
  408.4 3.2 copy-start.5
  436.4 3.4 copy-start.11
  436.4 3.4 copy-start.15
  542.4 16.5 %copy-start.33 = (f32[768]{0:T(1024)}, f32[768]{0:T(1024)S(1)}, u32[]{:S(2)}) copy-start(f32[768]{0:T(1024)S(1)} %slice.197) | copy-start | bytes 9220
  543.0 7.5 %copy-start.36 = (f32[768]{0:T(1024)S(1)}, f32[768]{0:T(1024)}, u32[]{:S(2)}) copy-start(f32[768]{0:T(1024)} %add.125) | copy-start | bytes 9220
  543.0 7.5 %copy-start.46 = (f32[4,256,768]{2,1,0:T(8,128)S(1)}, f32[4,256,768]{2,1,0:T(8,128)}, u32[]{:S(2)}) copy-start(f32[4,256,768]{2,1,0:T(8,128)} %fusion.6) | copy-start | bytes 9437188
  550.5 4.9 copy-start.31
  550.5 4.9 copy-start.32
  550.5 4.9 copy-start.4
  550.6 4.9 copy-start.6
  550.6 4.9 copy-start.10
  550.6 4.9 copy-start.26
  550.6 4.9 copy-start.30
  (9 other events, 18.9 us)
Sparse Core Ops, SparseCore 0:
  154.5 149.2 all-reduce.3
  350.0 185.1 all-reduce.5

commit v3 on v2

--- a/solution.py
+++ b/solution.py
@@ -15,17 +15,12 @@
 BF = jnp.bfloat16
 F32 = jnp.float32
 LOG2E = math.log2(math.e)
-TILE = 256
 
 
 def layer_norm(values, gain, bias):
     center = values - jnp.mean(values, axis=-1, keepdims=True)
     spread = jnp.mean(center * center, axis=-1, keepdims=True)
     return center * lax.rsqrt(spread + 1e-05) * gain + bias
-
-
-def gelu_exact(values):
-    return 0.5 * values * (1.0 + jax.scipy.special.erf(values * (1.0 / math.sqrt(2.0))))
 
 
 def rotary_rows(values, cosine, sine):
@@ -46,120 +41,461 @@
     return jnp.cos(angle), jnp.sin(angle)
 
 
+MESH = pl.DeviceIdType.MESH
+
+
 def dot(a, b, ca, cb):
     return lax.dot_general(a, b, (((ca,), (cb,)), ((), ())), preferred_element_type=F32)
 
 
+def flip(index, weight):
+    return index + weight - 2 * weight * lax.rem(index // weight, 2)
+
+
+def gelu_parts(u):
+    e = jnp.exp(u * u * -0.5)
+    t = 1.0 / (1.0 + (0.3275911 / math.sqrt(2.0)) * jnp.abs(u))
+    poly = t * (
+        0.5 * 0.254829592
+        + t
+        * (
+            0.5 * -0.284496736
+            + t * (0.5 * 1.421413741 + t * (0.5 * -1.453152027 + t * (0.5 * 1.061405429)))
+        )
+    )
+    tail = poly * e
+    return jnp.where(u >= 0, 1.0 - tail, tail), e * (1.0 / math.sqrt(2.0 * math.pi))
+
+
+def feed_kernel(
+    x_ref,
+    c_ref,
+    up_ref,
+    down_ref,
+    bias_ref,
+    ff_ref,
+    gx_ref,
+    gup_ref,
+    gdown_ref,
+    gbias_ref,
+    act_ref,
+    grad_ref,
+):
+    tokens = x_ref.shape[0]
+    bias = bias_ref[...]
+    sub = min(256, tokens)
+    for r in range(0, tokens, sub):
+        u = dot(x_ref[r : r + sub, :], up_ref[...], 1, 0) + bias
+        share, density = gelu_parts(u)
+        act_ref[r : r + sub, :] = (u * share).astype(BF)
+        da = dot(c_ref[r : r + sub, :], down_ref[...], 1, 1)
+        grad_ref[r : r + sub, :] = (da * (share + u * density)).astype(BF)
+
+    @pl.when(pl.program_id(0) == 0)
+    def _():
+        ff_ref[...] = jnp.zeros_like(ff_ref)
+        gx_ref[...] = jnp.zeros_like(gx_ref)
+
+    act, grad = act_ref[...], grad_ref[...]
+    ff_ref[...] += dot(act, down_ref[...], 1, 0)
+    gx_ref[...] += dot(grad, up_ref[...], 1, 1)
+    gdown_ref[...] = dot(act, c_ref[...], 0, 0).astype(BF)
+    gup_ref[...] = dot(x_ref[...], grad, 0, 0).astype(BF)
+    gbias_ref[...] = jnp.sum(grad.astype(F32), axis=0, keepdims=True)
+
+
+FEED_STEPS = 6
+
+
+def feed_forward(x, cot, up_weight, up_bias, down_weight):
+    tokens, d = x.shape
+    ff = up_weight.shape[1]
+    wide = ff // FEED_STEPS
+    whole = pl.BlockSpec((tokens, d), lambda i: (0, 0))
+    by_column = pl.BlockSpec((d, wide), lambda i: (0, i))
+    by_row = pl.BlockSpec((wide, d), lambda i: (i, 0))
+    line = pl.BlockSpec((1, wide), lambda i: (0, i))
+    return pl.pallas_call(
+        feed_kernel,
+        grid=(FEED_STEPS,),
+        out_shape=[
+            jax.ShapeDtypeStruct((tokens, d), F32),
+            jax.ShapeDtypeStruct((tokens, d), F32),
+            jax.ShapeDtypeStruct((d, ff), BF),
+            jax.ShapeDtypeStruct((ff, d), BF),
+            jax.ShapeDtypeStruct((1, ff), F32),
+        ],
+        in_specs=[whole, whole, by_column, by_row, line],
+        out_specs=[whole, whole, by_column, by_row, line],
+        scratch_shapes=[pltpu.VMEM((tokens, wide), BF), pltpu.VMEM((tokens, wide), BF)],
+        compiler_params=pltpu.CompilerParams(vmem_limit_bytes=56 * 2**20),
+        cost_estimate=pl.CostEstimate(
+            flops=12 * tokens * d * ff,
+            bytes_accessed=16 * d * ff,
+            transcendentals=tokens * ff,
+        ),
+        name="feed_forward",
+    )(x, cot, up_weight, down_weight, up_bias)
+
+
+KEYS = 256
+
+
+def shipped(upper_index, ring, tiles):
+    more = upper_index + 1
+    return (tiles * (2 * upper_index + 1 - ring) + more) // (2 * more)
+
+
 def attention_kernel(
-    q_ref, g_ref, k_ref, v_ref, kt_ref, vt_ref, o_ref, dq_ref, dk_ref, dv_ref, s_ref, p_ref
+    seqs,
+    groups,
+    q_ref,
+    g_ref,
+    all_ref,
+    att_ref,
+    dq_ref,
+    slot_ref,
+    kvt_ref,
+    flat_ref,
+    rows_ref,
+    dkv_ref,
+    s_ref,
+    p_ref,
+    qs_ref,
+    gs_ref,
+    qin_ref,
+    gin_ref,
+    atts_ref,
+    dqs_ref,
+    stage_ref,
+    half_ref,
+    load_sem,
+    own_sem,
+    in_send,
+    in_recv,
+    out_send,
+    out_recv,
+    core_send,
+    core_recv,
+    slot_send,
+    slot_recv,
 ):
     tiles, width, rows = q_ref.shape
+    ring = all_ref.shape[0]
+    chips = ring // 2
     heads = width // HEAD_DIM
     lanes = heads * rows
-    block = rows
-    dk_ref[...] = jnp.zeros_like(dk_ref)
-    dv_ref[...] = jnp.zeros_like(dv_ref)
-    keep = lax.broadcasted_iota(jnp.int32, (block, rows), 0) <= lax.broadcasted_iota(
-        jnp.int32, (block, rows), 1
-    )
-    keep = jnp.concatenate([keep] * heads, axis=1)
-
-    def side(ref, j):
-        return jnp.concatenate(
-            [ref[j, HEAD_DIM * h : HEAD_DIM * (h + 1), :] for h in range(heads)], axis=1
+    length = ring * rows
+    me = lax.axis_index("seq")
+    chip, core = me // 2, lax.rem(me, 2)
+    upper = me // chips
+    partner = ring - 1 - me
+    count = shipped(me + (1 - upper) * (partner - me), ring, tiles)
+
+    def to(index):
+        return {"seq": index}
+
+    barrier = pltpu.get_barrier_semaphore()
+
+    def greet(index):
+        pl.semaphore_signal(barrier, inc=1, device_id=to(index), device_id_type=MESH)
+
+    greet(partner)
+    greet(flip(me, 1))
+    for m in range(1, chips):
+        greet(lax.rem(me + 2 * m, ring))
+    pl.semaphore_wait(barrier, chips + 1)
+
+    def load(s, slot):
+        return pltpu.make_async_copy(
+            all_ref.at[:, pl.ds(pl.multiple_of(s * 2 * HEAD_DIM, 2 * HEAD_DIM), 2 * HEAD_DIM), :],
+            kvt_ref.at[slot],
+            load_sem.at[slot],
         )
 
-    def at(kb):
-        return pl.ds(pl.multiple_of(kb * block, block), block)
-
-    def tile(step, carry):
-        j = tiles - 1 - step
-        q = side(q_ref, j)
-        g = side(g_ref, j)
-
-        def scores(kb, top):
-            s = dot(k_ref[at(kb), :], q, 1, 0)
-            s_ref[at(kb), :] = s
-            return jnp.maximum(top, jnp.max(s, axis=0, keepdims=True))
-
-        s = jnp.where(keep, dot(k_ref[at(j), :], q, 1, 0), -1e30)
-        s_ref[at(j), :] = s
-        top = lax.fori_loop(0, j, scores, jnp.max(s, axis=0, keepdims=True))
-
-        def forward(kb, state):
+    load(0, 0).start()
+
+    def place(k):
+        return lax.rem(k, seqs) * groups + k // seqs
+
+    def remote(src, dst, sems, which, k, index):
+        return pltpu.make_async_remote_copy(
+            src_ref=src,
+            dst_ref=dst,
+            send_sem=sems[0].at[which, k],
+            recv_sem=sems[1].at[which, k],
+            device_id=to(index),
+            device_id_type=MESH,
+        )
+
+    def q_in(k):
+        return remote(q_ref.at[place(k)], qin_ref.at[k], (in_send, in_recv), 0, k, partner)
+
+    def g_in(k):
+        return remote(g_ref.at[place(k)], gin_ref.at[k], (in_send, in_recv), 1, k, partner)
+
+    def att_out(k):
+        return remote(atts_ref.at[k], att_ref.at[place(k)], (out_send, out_recv), 0, k, partner)
+
+    def dq_out(k):
+        return remote(dqs_ref.at[k], dq_ref.at[place(k)], (out_send, out_recv), 1, k, partner)
+
+    def start_in(k, carry):
+        q_in(k).start()
+        g_in(k).start()
+        return carry
+
+    lax.fori_loop(0, count * upper, start_in, 0)
+
+    def core_out(s):
+        return pltpu.make_async_remote_copy(
+            src_ref=stage_ref.at[s, :, 1 - core],
+            dst_ref=half_ref.at[s],
+            send_sem=core_send.at[s],
+            recv_sem=core_recv.at[s],
+            device_id=to(flip(me, 1)),
+            device_id_type=MESH,
+        )
+
+    def slot_out(s, m):
+        target = lax.rem(chip + m, chips)
+        return pltpu.make_async_remote_copy(
+            src_ref=half_ref.at[s, target],
+            dst_ref=slot_ref.at[s, m],
+            send_sem=slot_send.at[s, m],
+            recv_sem=slot_recv.at[s, m],
+            device_id=to(2 * target + core),
+            device_id_type=MESH,
+        )
+
+    def slot_own(s):
+        return pltpu.make_async_copy(half_ref.at[s, chip], slot_ref.at[s, 0], own_sem.at[s])
+
+    def pass_on(s):
+        core_out(s).wait_recv()
+
+        def add(m, carry):
+            half_ref[s, m] = (
+                half_ref[s, m].astype(F32) + stage_ref[s, m, core].astype(F32)
+            ).astype(BF)
+            return carry
+
+        lax.fori_loop(0, chips, add, 0)
+        slot_own(s).start()
+        for m in range(1, chips):
+            slot_out(s, m).start()
+
+    qs_ref[...] = jnp.zeros_like(qs_ref)
+    gs_ref[...] = jnp.zeros_like(gs_ref)
+
+    def at(b, n=1):
+        return pl.ds(pl.multiple_of(b * KEYS, KEYS), n * KEYS)
+
+    def blocks(count_blocks, body, state):
+        state = lax.fori_loop(0, count_blocks // 4, lambda i, c: body(4 * i, 4, c), state)
+        pairs = count_blocks // 2
+        state = lax.fori_loop(
+            count_blocks // 4 * 2, pairs, lambda i, c: body(2 * i, 2, c), state
+        )
+        return lax.fori_loop(2 * pairs, count_blocks, lambda i, c: body(i, 1, c), state)
+
+    def tile(q_tile, g_tile, att_tile, dq_tile, position):
+        start = position * rows
+        edge = start // KEYS
+        shift = lax.rem(start, KEYS)
+        for h in range(heads):
+            qs_ref[0:HEAD_DIM, h * rows : (h + 1) * rows] = q_tile[
+                h * HEAD_DIM : (h + 1) * HEAD_DIM, :
+            ]
+        s = dot(rows_ref[at(edge), :], qs_ref[...], 1, 0)
+        column = lax.rem(lax.broadcasted_iota(jnp.int32, (1, lanes), 1), rows) + shift
+        keep = lax.broadcasted_iota(jnp.int32, (KEYS, lanes), 0) <= column
+        s = jnp.where(keep, s, -1e30)
+        s_ref[at(edge), :] = s
+
+        def top_of(s, n):
+            return jnp.max(s.reshape(n * KEYS // 8, 8, lanes), axis=0)
+
+        def scores(b, n, top):
+            s = dot(rows_ref[at(b, n), :], qs_ref[...], 1, 0)
+            s_ref[at(b, n), :] = s
+            return jnp.maximum(top, top_of(s, n))
+
+        top = jnp.max(blocks(edge, scores, top_of(s, 1)), axis=0, keepdims=True)
+
+        def forward(b, n, state):
             total, out = state
-            p = jnp.exp2(s_ref[at(kb), :] - top)
+            p = jnp.exp2(s_ref[at(b, n), :] - top)
             low = p.astype(BF)
-            p_ref[at(kb), :] = low
+            p_ref[at(b, n), :] = low
             return (
-                total + jnp.sum(p, axis=0, keepdims=True),
-                out + dot(vt_ref[:, at(kb)], low, 1, 0),
+                total + jnp.sum(p.reshape(n * KEYS // 8, 8, lanes), axis=0),
+                out + dot(flat_ref[HEAD_DIM : 2 * HEAD_DIM, at(b, n)], low, 1, 0),
             )
 
-        total, out = lax.fori_loop(
-            0,
-            j + 1,
-            forward,
-            (jnp.zeros((1, lanes), F32), jnp.zeros((HEAD_DIM, lanes), F32)),
+        total, out = blocks(
+            edge + 1, forward, (jnp.zeros((8, lanes), F32), jnp.zeros((HEAD_DIM, lanes), F32))
         )
-        inverse = 1.0 / total
+        inverse = 1.0 / jnp.sum(total, axis=0, keepdims=True)
         out = out * inverse
-        scaled = (g.astype(F32) * inverse).astype(BF)
-        delta = jnp.sum(scaled.astype(F32) * out, axis=0, keepdims=True)
-        high = delta.astype(BF)
-        rest = delta - high.astype(F32)
-        middle = rest.astype(BF)
-        last = (rest - middle.astype(F32)).astype(BF)
-        stacked = jnp.concatenate(
-            [scaled, high, middle, last, jnp.zeros((13, lanes), BF)], axis=0
-        )
         for h in range(heads):
-            o_ref[j, HEAD_DIM * h : HEAD_DIM * (h + 1), :] = out[
+            att_tile[h * HEAD_DIM : (h + 1) * HEAD_DIM, :] = out[
                 :, h * rows : (h + 1) * rows
             ].astype(BF)
-
-        def backward(kb, dq):
-            p = p_ref[at(kb), :]
-            dp = dot(v_ref[at(kb), :], stacked, 1, 0)
-            ds = (p.astype(F32) * dp).astype(BF)
-            dv_ref[at(kb), :] += dot(p, scaled, 1, 1)
-            dk_ref[at(kb), :] += dot(ds, q, 1, 1)
-            return dq + dot(kt_ref[:, at(kb)], ds, 1, 0)
-
-        dq = lax.fori_loop(0, j + 1, backward, jnp.zeros((HEAD_DIM, lanes), F32))
+        g = jnp.concatenate(
+            [g_tile[h * HEAD_DIM : (h + 1) * HEAD_DIM, :] for h in range(heads)], axis=1
+        )
+        scaled = (g.astype(F32) * inverse).astype(BF)
+        gs_ref[HEAD_DIM : 2 * HEAD_DIM, :] = scaled
+        delta = jnp.sum(scaled.astype(F32) * out, axis=0, keepdims=True)
+
+        def backward(b, n, dq):
+            p = p_ref[at(b, n), :]
+            dp = dot(rows_ref[at(b, n), :], gs_ref[...], 1, 0)
+            ds = (p.astype(F32) * (dp - delta)).astype(BF)
+            dkv_ref[at(b, n), :] += dot(p, gs_ref[...], 1, 1) + dot(ds, qs_ref[...], 1, 1)
+            return dq + dot(flat_ref[0:HEAD_DIM, at(b, n)], ds, 1, 0)
+
+        dq = blocks(edge + 1, backward, jnp.zeros((HEAD_DIM, lanes), F32))
         dq = dq * (HEAD_DIM**-0.5)
         for h in range(heads):
-            dq_ref[j, HEAD_DIM * h : HEAD_DIM * (h + 1), :] = dq[
+            dq_tile[h * HEAD_DIM : (h + 1) * HEAD_DIM, :] = dq[
                 :, h * rows : (h + 1) * rows
             ].astype(BF)
+
+    per_block = KEYS // rows
+
+    def sequence(s, carry):
+        slot = lax.rem(s, 2)
+        load(s, slot).wait()
+        pl.when(s + 1 < seqs)(lambda: load(s + 1, 1 - slot).start())
+        dkv_ref[...] = jnp.zeros_like(dkv_ref)
+
+        def turn(b, c):
+            wide = jnp.concatenate(
+                [kvt_ref[slot, b * per_block + i] for i in range(per_block)], axis=1
+            )
+            flat_ref[:, at(b)] = wide
+            rows_ref[at(b), :] = wide.T
+            return c
+
+        lax.fori_loop(0, length // KEYS, turn, 0)
+        given = (count - s + seqs - 1) // seqs
+        own = groups - upper * given
+        taken = (1 - upper) * given
+        later = jnp.minimum(s, 1)
+
+        def work(u, c):
+            v = u - taken * later
+            mine = (v >= 0) & (v < own)
+
+            @pl.when(mine)
+            def _():
+                t = s * groups + upper * given + v
+                tile(q_ref.at[t], g_ref.at[t], att_ref.at[t], dq_ref.at[t], me)
+
+            @pl.when(jnp.logical_not(mine))
+            def _():
+                k = (u - own * (1 - later)) * seqs + s
+                q_in(k).wait_recv()
+                g_in(k).wait_recv()
+                tile(qin_ref.at[k], gin_ref.at[k], atts_ref.at[k], dqs_ref.at[k], partner)
+                att_out(k).start()
+                dq_out(k).start()
+
+            pl.when((u == 0) & (s > 0))(lambda: pass_on(s - 1))
+            return c
+
+        lax.fori_loop(0, own + taken, work, 0)
+        stage_ref[s] = dkv_ref[...].reshape(chips, 2, rows, 2 * HEAD_DIM).astype(BF)
+        core_out(s).start()
         return carry
 
-    lax.fori_loop(0, tiles, tile, 0)
-
-
-def attention(q, g, key, value):
+    lax.fori_loop(0, seqs, sequence, 0)
+    pass_on(seqs - 1)
+
+    def end_given(k, c):
+        q_in(k).wait_send()
+        g_in(k).wait_send()
+        att_out(k).wait_recv()
+        dq_out(k).wait_recv()
+        return c
+
+    def end_taken(k, c):
+        att_out(k).wait_send()
+        dq_out(k).wait_send()
+        return c
+
+    lax.fori_loop(0, count * upper, end_given, 0)
+    lax.fori_loop(0, count * (1 - upper), end_taken, 0)
+
+    def end(s, c):
+        core_out(s).wait_send()
+        slot_own(s).wait()
+        for m in range(1, chips):
+            slot_out(s, m).wait()
+        return c
+
+    lax.fori_loop(0, seqs, end, 0)
+
+
+def attention(q, g, kv_all, seqs):
     tiles, width, rows = q.shape
-    length = tiles * rows
+    ring = kv_all.shape[0]
+    chips = ring // 2
+    length = ring * rows
     lanes = width // HEAD_DIM * rows
-    ones = jnp.concatenate([jnp.full((length, 3), -1, BF), jnp.zeros((length, 13), BF)], axis=1)
-    whole = pl.BlockSpec(memory_space=pltpu.VMEM)
-    flops = 12 * length * length // 2 * width
+    most = max(shipped(i, ring, tiles) for i in range(chips, ring))
+    vmem = pl.BlockSpec(memory_space=pltpu.VMEM)
+    anywhere = pl.BlockSpec(memory_space=pl.ANY)
+    pair = 2 * HEAD_DIM
+    dma = pltpu.SemaphoreType.DMA
     return pl.pallas_call(
-        attention_kernel,
-        out_shape=[jax.ShapeDtypeStruct(q.shape, BF)] * 2
-        + [jax.ShapeDtypeStruct((length, HEAD_DIM), F32)] * 2,
-        in_specs=[whole] * 6,
-        out_specs=[whole] * 4,
-        scratch_shapes=[pltpu.VMEM((length, lanes), F32), pltpu.VMEM((length, lanes), BF)],
-        compiler_params=pltpu.CompilerParams(vmem_limit_bytes=56 * 2**20),
+        functools.partial(attention_kernel, seqs, tiles // seqs),
+        out_shape=[
+            jax.ShapeDtypeStruct(q.shape, BF),
+            jax.ShapeDtypeStruct(q.shape, BF),
+            jax.ShapeDtypeStruct((seqs, chips, rows, pair), BF),
+        ],
+        in_specs=[vmem, vmem, anywhere],
+        out_specs=[vmem, vmem, anywhere],
+        scratch_shapes=[
+            pltpu.VMEM((2, ring, pair, rows), BF),
+            pltpu.VMEM((pair, length), BF),
+            pltpu.VMEM((length, pair), BF),
+            pltpu.VMEM((length, pair), F32),
+            pltpu.VMEM((length, lanes), F32),
+            pltpu.VMEM((length, lanes), BF),
+            pltpu.VMEM((pair, lanes), BF),
+            pltpu.VMEM((pair, lanes), BF),
+            pltpu.VMEM((most, width, rows), BF),
+            pltpu.VMEM((most, width, rows), BF),
+            pltpu.VMEM((most, width, rows), BF),
+            pltpu.VMEM((most, width, rows), BF),
+            pltpu.VMEM((seqs, chips, 2, rows, pair), BF),
+            pltpu.VMEM((seqs, chips, rows, pair), BF),
+            dma((2,)),
+            dma((seqs,)),
+            dma((2, most)),
+            dma((2, most)),
+            dma((2, most)),
+            dma((2, most)),
+            dma((seqs,)),
+            dma((seqs,)),
+            dma((seqs, chips)),
+            dma((seqs, chips)),
+        ],
+        compiler_params=pltpu.CompilerParams(
+            collective_id=2, has_side_effects=True, vmem_limit_bytes=58 * 2**20
+        ),
         cost_estimate=pl.CostEstimate(
-            flops=flops, bytes_accessed=4 * q.size, transcendentals=length * length // 2 * 3
+            flops=12 * tiles * rows * width * length * 4,
+            bytes_accessed=8 * q.size,
+            transcendentals=tiles * lanes * length // 2,
         ),
         name="attention",
-    )(q, g, key, jnp.concatenate([value, ones], axis=1), key.T, value.T)
-
-
-MESH=pl.DeviceIdType.MESH
+    )(q, g, kv_all)
+
 
 def bit_orders(dp, ring):
     seq_bits = [("seq", 1 << b) for b in range(ring.bit_length() - 1)]
@@ -290,7 +626,6 @@
     groups = ring // seq_count
     per_group = HEADS // groups
     width = per_group * HEAD_DIM
-    length = ring * local_len
     hidden = hidden_in.astype(F32)
     cosine, sine = angles_of(positions)
     normed_a, pull_a = jax.vjp(layer_norm, hidden, ln1_gain, ln1_bias)
@@ -298,9 +633,7 @@
     normed_a = normed_a.astype(BF)
     normed_m = normed_m.astype(BF)
 
-    def swap(x):
-        return lax.all_to_all(x, "seq", split_axis=0, concat_axis=0, tiled=True)
-
+    tokens = seq_count * local_len
     kv_weight = jnp.concatenate([shared_key_weight, shared_value_weight], axis=1)
     kv_bias = jnp.concatenate([shared_key_bias, shared_value_bias])
     kv_pre = jnp.einsum("stc,cw->swt", normed_a, kv_weight, preferred_element_type=F32)
@@ -308,68 +641,41 @@
     kv_low = jnp.concatenate(
         [rotary_rows(kv_pre[:, :HEAD_DIM], cosine, sine), kv_pre[:, HEAD_DIM:]], axis=1
     ).astype(BF)
-    kv_send = jnp.broadcast_to(
-        kv_low[:, None], (seq_count, groups, 2 * HEAD_DIM, local_len)
-    ).reshape(ring, 2 * HEAD_DIM, local_len)
+    kv_all = lax.all_gather(kv_low.reshape(-1, local_len), "seq")
     query_pre = jnp.einsum("stc,cw->swt", normed_a, query_projection, preferred_element_type=F32)
     query_pre = (query_pre + query_bias[:, None]).reshape(seq_count, HEADS, HEAD_DIM, local_len)
     query_low = (rotary_rows(query_pre, cosine[:, None], sine[:, None]) * (LOG2E / 8.0)).astype(BF)
-    query_send = query_low.reshape(ring, width, local_len)
+    query_tiles = query_low.reshape(-1, width, local_len)
     grad_attended = jnp.einsum(
         "stc,wc->swt", cotangent, output_weight, preferred_element_type=F32
     ).astype(BF)
-    grad_send = grad_attended.reshape(ring, width, local_len)
-    query_send, kv_send, grad_send = lax.optimization_barrier((query_send, kv_send, grad_send))
-    kv_here = swap(kv_send)
-    query_here = swap(query_send)
-    grad_here = swap(grad_send)
-
-    up_pre = jnp.einsum("stc,cf->stf", normed_m, up_weight, preferred_element_type=F32) + up_bias
-    activation, pull_gelu = jax.vjp(gelu_exact, up_pre)
-    activation = activation.astype(BF)
-    feedforward = jnp.einsum(
-        "stf,fc->stc", activation, down_weight, preferred_element_type=F32
-    )
-    activation_gradient = jnp.einsum(
-        "stc,fc->stf", cotangent, down_weight, preferred_element_type=F32
-    )
-    grad_up = pull_gelu(activation_gradient)[0].astype(BF)
-    grad_w_down = jnp.einsum(
-        "stf,stc->fc", activation, cotangent, preferred_element_type=F32
-    ).astype(BF)
-    grad_w_up = jnp.einsum("stc,stf->cf", normed_m, grad_up, preferred_element_type=F32).astype(BF)
-    grad_normed_m = jnp.einsum("stf,cf->stc", grad_up, up_weight, preferred_element_type=F32)
-    kv_here, query_here, grad_here, grad_w_up, grad_w_down, feedforward, grad_normed_m = lax.optimization_barrier(
-        (kv_here, query_here, grad_here, grad_w_up, grad_w_down, feedforward, grad_normed_m)
+    grad_tiles = grad_attended.reshape(-1, width, local_len)
+
+    feedforward, grad_normed_m, grad_w_up, grad_w_down, grad_b_up = feed_forward(
+        normed_m.reshape(tokens, D),
+        cotangent.reshape(tokens, D),
+        up_weight,
+        up_bias[None],
+        down_weight,
+    )
+    feedforward = feedforward.reshape(hidden.shape)
+    grad_normed_m = grad_normed_m.reshape(hidden.shape)
+    grad_b_up = grad_b_up[0]
+    grad_b_down = jnp.sum(cotangent.astype(F32), axis=(0, 1))
+    query_tiles, grad_tiles, kv_all, grad_w_up, grad_w_down = lax.optimization_barrier(
+        (query_tiles, grad_tiles, kv_all, grad_w_up, grad_w_down)
     )
     grad_w_down = lax.psum(grad_w_down, ("dp", "seq"))
-    grad_b_up = jnp.sum(grad_up.astype(F32), axis=(0, 1))
-    grad_b_down = jnp.sum(cotangent.astype(F32), axis=(0, 1))
-
-    def to_tiles(x):
-        tile_len = max(TILE, local_len)
-        x = x.reshape(length // tile_len, tile_len // local_len, width, local_len)
-        return x.transpose(0, 2, 1, 3).reshape(length // tile_len, width, tile_len)
-
-    def from_tiles(x):
-        tile_len = max(TILE, local_len)
-        x = x.reshape(length // tile_len, width, tile_len // local_len, local_len)
-        return x.transpose(0, 2, 1, 3).reshape(ring, width, local_len)
-
-    kv_rows = kv_here.transpose(0, 2, 1).reshape(length, 2 * HEAD_DIM)
-    out, dq, dk, dv = attention(
-        to_tiles(query_here), to_tiles(grad_here), kv_rows[:, :HEAD_DIM], kv_rows[:, HEAD_DIM:]
-    )
-    out, dq, dk, dv, grad_w_up, grad_w_down = lax.optimization_barrier(
-        (out, dq, dk, dv, grad_w_up, grad_w_down)
+    out, dq, dkv = attention(query_tiles, grad_tiles, kv_all, seq_count)
+    out, dq, dkv, grad_w_up, grad_w_down = lax.optimization_barrier(
+        (out, dq, dkv, grad_w_up, grad_w_down)
     )
     grad_w_up = lax.psum(grad_w_up, ("dp", "seq"))
-    attended = swap(from_tiles(out)).reshape(seq_count, D, local_len)
-    query_back = swap(from_tiles(dq)).reshape(seq_count, HEADS, HEAD_DIM, local_len)
-    kv_part = jnp.concatenate([dk * (1.0 / LOG2E), dv], axis=1).astype(BF)
-    kv_back = swap(kv_part.reshape(ring, local_len, 2 * HEAD_DIM)).astype(F32)
-    kv_grad = jnp.sum(kv_back.reshape(seq_count, groups, local_len, 2 * HEAD_DIM), axis=1)
-    kv_grad = kv_grad.astype(BF).astype(F32).transpose(0, 2, 1)
+    attended = out.reshape(seq_count, D, local_len)
+    query_back = dq.reshape(seq_count, HEADS, HEAD_DIM, local_len)
+    kv_grad = jnp.sum(dkv.astype(F32), axis=1)
+    kv_scale = jnp.concatenate([jnp.full((HEAD_DIM,), 1.0 / LOG2E), jnp.ones((HEAD_DIM,))])
+    kv_grad = (kv_grad * kv_scale).astype(BF).astype(F32).transpose(0, 2, 1)
 
     attention_out = jnp.einsum(
         "swt,wc->stc", attended, output_weight, preferred_element_type=F32

time: 570 us -> 511 us (0.90); the launches traced: 567 us -> 501 us
  Pallas kernels: 205 us -> 296 us
  matrix products: 86.4 us -> 22.3 us
  starting transfers between devices: 49.7 us -> 0.12 us
  blocking collectives: 30 us -> 0 us
  local copies, waits for them, and re-layouts: 44.2 us -> 30 us
    pallas_call x1 -> x2, Pallas kernels: 143 us -> 231 us  [the longest x1 190 us: attention(): pl.pallas_call(functools.partial(attention_kernel, seqs, tiles // seqs),...]
    dot_general x6 -> x0, matrix products: 61.8 us -> none  [the longest x1 13.9 us: local(): jnp.einsum('stc,fc->stf', cotangent, down_weight, preferred_element_type=...]
    all_to_all x5 -> x0, waiting for transfers between devices: 53.9 us -> none  [swap(): return lax.all_to_all(x, 'seq', split_axis=0, concat_axis=0, tiled=True)]
    all_to_all x5 -> x0, starting transfers between devices: 49.6 us -> none  [swap(): return lax.all_to_all(x, 'seq', split_axis=0, concat_axis=0, tiled=True)]
    psum x1, waiting for transfers between devices: 31.4 us -> 61.6 us  [local(): grad_w_up = lax.psum(grad_w_up, ('dp', 'seq'))]
    all_to_all x1 -> x0, blocking collectives: 30 us -> none  [swap(): return lax.all_to_all(x, 'seq', split_axis=0, concat_axis=0, tiled=True)]
    psum x1, waiting for transfers between devices: 4.04 us -> 27.8 us  [local(): grad_w_down = lax.psum(grad_w_down, ('dp', 'seq'))]
    unnamed x109 -> x123, local copies, waits for them, and re-layouts: 12.8 us -> 5.83 us
  transfers between devices with their start and end apart: 7 -> 3, of which waited for: 5 -> 2; matrix products, arithmetic and copies ran while one was open for 22% -> 9% of each run, Pallas kernels for 36% -> 59%
where the time goes in v3:
time: 511 us; the launch traced here: 501 us
  Pallas kernels  296 us (58%)
  waiting for transfers between devices  89.4 us (17%)
  other arithmetic  48.2 us (9%)
  local copies, waits for them, and re-layouts  30 us (6%)
  matrix products  22.3 us (4%)
  between operations  14.9 us (3%)
    pallas_call x1, Pallas kernels, attention(): pl.pallas_call(functools.partial(attention_kernel, seqs, tiles // seqs),...  190 us
    pallas_call x1, Pallas kernels, total_of(): pl.pallas_call(functools.partial(sum_kernel, orders), out_shape=jax.Shape...  65.2 us
    psum x1, waiting for transfers between devices, local(): grad_w_up = lax.psum(grad_w_up, ('dp', 'seq'))  61.6 us
    pallas_call x1, Pallas kernels, feed_forward(): pl.pallas_call(feed_kernel, grid=(FEED_STEPS,), out_shape=[jax.ShapeDtype...  41.2 us
    psum x1, waiting for transfers between devices, local(): grad_w_down = lax.psum(grad_w_down, ('dp', 'seq'))  27.8 us
  transfers between devices with their start and end apart: 3, of which 2 were waited for; matrix products, arithmetic and copies ran while one was open for 9% of the time, Pallas kernels for 59%

profile of v3, /device:TPU:0, one launch (start us, length us, event | category | flops | bytes accessed | tf_op | source)
XLA Modules:
  0.0 501.0 jit_solution(14208226672116545247)
XLA Ops:
  7.4 1.8 convert_reduce_fusion
  9.2 2.0 fusion.16
  11.9 0.9 fusion.27
  12.9 0.8 fusion.43
  13.8 0.7 pad_maximum_fusion.3
  14.6 0.8 copy.71
  15.4 0.8 copy.70
  16.2 4.6 add_bitcast_fusion
  20.8 3.5 copy.63
  24.3 3.4 slice.163
  28.3 2.3 reduce.2
  30.6 1.8 fusion.13
  32.4 41.2 %feed_forward.1 = (f32[1024,768]{1,0:T(8,128)}, f32[1024,768]{1,0:T(8,128)}, bf16[768,3072]{1,0:T(8,128)(2,1)}, bf16[3072,768]{1,0:T(8,128)(2,1)}, f32[1,3072]{1,0:T(1,128)}) custom-call(bf16[1024,768]{1,0:T(8,128)(2,1)} %bitcast.63, bf16[1024,768]{1,0:T(8,128)(2,1)} %bitcast.57, bf16[768,3072]{1,0:T(8,128)(2,1)} %up_ref.1, bf16[3072,768]{1,0:T(8,128)(2,1)} %down_ref.1, ...), custom_call_target="tpu_custom_call" | custom-call | flops 28991029248 | bytes 37748736 | tf_op jit(solution)/shard_map/feed_forward/pallas_call | solution.py:118
  73.6 2.9 reduce_sum.132
  76.4 0.6 convert_reduce_fusion.2
  77.1 1.3 multiply_subtract_fusion
  78.4 1.6 fusion.21
  80.0 2.6 convolution_convert_fusion
  82.6 189.7 %attention.1 = (bf16[16,192,256]{2,1,0:T(8,128)(2,1)}, bf16[16,192,256]{2,1,0:T(8,128)(2,1)}, bf16[4,8,256,128]{3,2,1,0:T(8,128)(2,1)}) custom-call(bf16[16,192,256]{2,1,0:T(8,128)(2,1)} %bitcast.64, bf16[16,192,256]{2,1,0:T(8,128)(2,1)} %bitcast.70, bf16[16,512,256]{2,1,0:T(8,128)(2,1)} %all-gather.2.cloned.1.call-done.all_ref), custom_call_target="tpu_custom_call" | custom-call | flops 154618822656 | bytes 6291456 | tf_op jit(solution)/shard_map/attention/pallas_call | solution.py:453
  272.3 27.8 %all-reduce.4.cloned.1.call-done = bf16[3072,768]{1,0:T(8,128)(2,1)} async-done(((bf16[3072,768]{1,0:T(8,128)(2,1)}), bf16[3072,768]{1,0:T(8,128)(2,1)}) %all-reduce.4.cloned.1.call-update) | async-done | bytes 4718608 | tf_op jit(solution)/shard_map/psum | solution.py:668
  300.1 2.5 slice.169
  302.6 2.1 convert_element_type.101
  305.2 0.9 fusion.59
  306.4 1.0 fusion.51
  307.7 1.2 subtract_convert_fusion
  309.0 1.4 pad_maximum_fusion.2
  310.3 2.7 copy.66
  313.0 2.5 fusion.57
  315.6 4.8 bitcast_convert_fusion
  320.5 2.8 fusion.58
  323.3 2.5 fusion.14
  327.7 2.4 slice.173
  330.1 2.4 copy.75
  332.5 0.9 slice_bitcast_fusion.2
  333.4 3.4 bitcast_convert_fusion.1
  336.9 1.9 pad_maximum_fusion.x_ref
  338.8 65.2 %total.1 = bf16[1792,768]{1,0:T(8,128)(2,1)} custom-call(bf16[1792,768]{1,0:T(8,128)(2,1)} %pad_maximum_fusion.x_ref), custom_call_target="tpu_custom_call" | custom-call | tf_op jit(solution)/shard_map/total/pallas_call | solution.py:595
  404.1 4.7 convert_element_type.110
  408.8 3.3 fusion.20
  412.4 0.9 copy-done.10
  413.3 3.4 add_add_fusion.2
  416.7 61.6 %all-reduce.6.cloned.1.call-done = bf16[768,3072]{1,0:T(8,128)(2,1)} async-done(((bf16[768,3072]{1,0:T(8,128)(2,1)}), bf16[768,3072]{1,0:T(8,128)(2,1)}) %all-reduce.6.cloned.1.call-update) | async-done | bytes 4718608 | tf_op jit(solution)/shard_map/psum | solution.py:673
  478.2 2.3 convert_element_type.108
  480.8 2.5 fusion.61
  483.4 0.6 slice_reduce_fusion
  484.0 0.8 slice_bitcast_fusion
  485.4 0.6 slice.188
  486.0 7.4 %convert_element_type.109 = f32[768,3072]{1,0:T(8,128)} convert(bf16[768,3072]{1,0:T(8,128)(2,1)} %all-reduce.6.cloned.1.call-done) | non-fusion elementwise | flops 2359296 | bytes 14155776 | tf_op jit(solution)/shard_map/convert_element_type | solution.py:753
  (151 shorter events, 6.3 us)
Async XLA Ops:
  7.2 72.8 %copy-start = (bf16[768,768]{1,0:T(8,128)(2,1)S(1)}, bf16[768,768]{1,0:T(8,128)(2,1)}, u32[]{:S(2)}) copy-start(bf16[768,768]{1,0:T(8,128)(2,1)} %param.31) | copy-start | bytes 3538948
  7.2 4.7 copy-start.4
  7.2 4.0 copy-start.43
  7.2 4.6 copy-start.51
  7.2 4.6 copy-start.52
  7.2 4.7 copy-start.50
  7.3 4.6 copy-start.31
  7.3 4.6 copy-start.20
  7.3 4.6 copy-start.21
  7.3 75.2 %all-gather.2.cloned.1.call-start = ((), (), s32[]{:S(2)}) async-start(), calls=%async_computation | async-start | bytes 4456448 | tf_op jit(solution)/shard_map/all_gather | solution.py:644
  7.4 5.6 %copy-start.44 = (f32[8]{0:T(128)}, f32[8]{0:T(128)S(1)}, u32[]{:S(2)}) copy-start(f32[8]{0:T(128)S(1)} %multiply_exponential_fusion) | copy-start | bytes 100
  9.2 21.4 %copy-start.18 = (f32[4,256]{1,0:T(4,128)}, f32[4,256]{1,0:T(4,128)S(1)}, u32[]{:S(2)}) copy-start(f32[4,256]{1,0:T(4,128)S(1)} %broadcast_multiply_fusion) | copy-start | bytes 12292
  11.2 19.3 %copy-start.22 = (f32[4,256]{1,0:T(4,128)}, f32[4,256]{1,0:T(4,128)S(1)}, u32[]{:S(2)}) copy-start(f32[4,256]{1,0:T(4,128)S(1)} %fusion.54) | copy-start | bytes 12292
  11.9 4.3 copy-start.49
  14.5 285.6 %all-reduce.4.cloned.1.call-start = ((), (), s32[]{:S(2)}) async-start(), calls=%async_computation.1 | async-start | bytes 9437184 | tf_op jit(solution)/shard_map/psum | solution.py:668
  24.3 3.4 copy-start.40
  24.3 3.4 copy-start.41
  24.3 6.3 %copy-start.24 = (f32[768]{0:T(1024)S(1)}, f32[768]{0:T(1024)}, u32[]{:S(2)}) copy-start(f32[768]{0:T(1024)} %param.23) | copy-start | bytes 9220
  24.3 6.3 %copy-start.39 = (f32[768]{0:T(1024)S(1)}, f32[768]{0:T(1024)}, u32[]{:S(2)}) copy-start(f32[768]{0:T(1024)} %param.24) | copy-start | bytes 9220
  73.6 4.8 copy-start.8
  82.6 395.7 %all-reduce.6.cloned.1.call-start = ((), (), s32[]{:S(2)}) async-start(), calls=%async_computation.2 | async-start | bytes 9437184 | tf_op jit(solution)/shard_map/psum | solution.py:673
  272.3 30.3 %copy-start.12 = (bf16[16,192,256]{2,1,0:T(8,128)(2,1)S(1)}, bf16[16,192,256]{2,1,0:T(8,128)(2,1)}, u32[]{:S(2)}) copy-start(bf16[16,192,256]{2,1,0:T(8,128)(2,1)} %get-tuple-element.50) | copy-start | bytes 4718596
  300.1 4.6 copy-start.15
  305.0 3.9 copy-start.13
  310.3 5.2 %copy-start.5 = (bf16[4,256,768]{2,1,0:T(8,128)(2,1)S(1)}, bf16[4,256,768]{2,1,0:T(8,128)(2,1)}, u32[]{:S(2)}) copy-start(bf16[4,256,768]{2,1,0:T(8,128)(2,1)} %param.19) | copy-start | bytes 4718596
  310.3 5.2 %copy-start.19 = (f32[4,256]{1,0:T(4,128)S(1)}, f32[4,256]{1,0:T(4,128)}, u32[]{:S(2)}) copy-start(f32[4,256]{1,0:T(4,128)} %copy-done.18) | copy-start | bytes 12292
  310.3 5.2 %copy-start.23 = (f32[4,256]{1,0:T(4,128)S(1)}, f32[4,256]{1,0:T(4,128)}, u32[]{:S(2)}) copy-start(f32[4,256]{1,0:T(4,128)} %copy-done.22) | copy-start | bytes 12292
  310.3 5.2 %copy-start.32 = (f32[768]{0:T(1024)S(1)}, f32[768]{0:T(1024)}, u32[]{:S(2)}) copy-start(f32[768]{0:T(1024)} %param.21) | copy-start | bytes 9220
  315.6 4.9 copy-start.1
  315.6 4.8 copy-start.11
  315.6 4.8 copy-start.16
  315.6 4.8 copy-start.17
  315.6 4.8 copy-start.25
  315.6 4.8 copy-start.48
  323.3 3.3 copy-start.37
  323.3 3.5 copy-start.38
  323.3 3.7 copy-start.30
  323.3 3.9 copy-start.36
  333.4 3.4 copy-start.14
  333.4 70.6 %slice-start = ((s8[4718592]{0:T(1024)(128)(4,1)}), s8[4194304]{0:T(1024)(128)(4,1)S(1)}, s32[]{:S(2)}) async-start(s8[4718592]{0:T(1024)(128)(4,1)} %bitcast.61), calls=%async_computation.3 | async-start | bytes 8388608
  336.9 67.1 %slice-start.1 = ((s8[4718592]{0:T(1024)(128)(4,1)}), s8[524288]{0:T(1024)(128)(4,1)S(1)}, s32[]{:S(2)}) async-start(s8[4718592]{0:T(1024)(128)(4,1)} %bitcast.61), calls=%async_computation.4 | async-start | bytes 1048576
  404.0 4.7 copy-start.42
  404.0 4.7 copy-start.53
  404.0 4.7 copy-start.54
  408.8 3.3 copy-start.2
  408.8 3.6 copy-start.7
  408.8 4.5 copy-start.10
  485.4 8.0 %copy-start.33 = (f32[768]{0:T(1024)}, f32[768]{0:T(1024)S(1)}, u32[]{:S(2)}) copy-start(f32[768]{0:T(1024)S(1)} %slice.187) | copy-start | bytes 9220
  (12 other events, 28.5 us)
Sparse Core Ops, SparseCore 0:
  14.6 53.2 all-gather.1
  82.7 217.3 all-reduce.3
  332.6 145.5 all-reduce.5

commit v4 on v3

--- a/solution.py
+++ b/solution.py
@@ -142,19 +142,130 @@
 
 
 def shipped(upper_index, ring, tiles):
-    more = upper_index + 1
+    more = upper_index + 2
     return (tiles * (2 * upper_index + 1 - ring) + more) // (2 * more)
+
+
+class Exchange:
+    def __init__(self, index, order, array, out, acc, recv, first, wide, sems):
+        self.index, self.order, self.sems = index, order, sems
+        self.array, self.out, self.acc, self.recv = array, out, acc, recv
+        self.columns = pl.ds(first, wide)
+        self.rows = array.shape[0]
+        self.halvings = halvings_of(self.rows, len(order))
+        self.waits = len(order) + self.halvings
+
+    def size(self, s):
+        return self.rows >> min(s, self.halvings)
+
+    def base(self, s):
+        return sum(self.size(t + 1) for t in range(s))
+
+    def start(self, s, first=1):
+        at = 0
+        for t in range(first, min(s, self.halvings)):
+            at = at + side_of(self.order[t]) * self.size(t + 1)
+        return at
+
+    def copy(self, k):
+        stages = len(self.order)
+        if k < stages:
+            bit = self.order[k]
+            size = self.size(k + 1)
+            other = self.start(k) + ((1 - side_of(bit)) * size if k < self.halvings else 0)
+            rows = pl.ds(pl.multiple_of(other, size), size)
+            src = (self.array if k == 0 else self.acc).at[rows, self.columns]
+            dst = self.recv.at[pl.ds(self.base(k), size), self.columns]
+        else:
+            t = self.waits - 1 - k
+            bit = self.order[t]
+            size = self.size(t + 1)
+            rows = pl.ds(pl.multiple_of(self.start(t + 1, 0), size), size)
+            src = dst = self.out.at[rows, self.columns]
+        return pltpu.make_async_remote_copy(
+            src_ref=src,
+            dst_ref=dst,
+            send_sem=self.sems[0].at[self.index, k],
+            recv_sem=self.sems[1].at[self.index, k],
+            device_id=partner_of(bit),
+            device_id_type=MESH,
+        )
+
+    def fill(self):
+        half = self.size(1)
+        rows = pl.ds(pl.multiple_of(side_of(self.order[0]) * half, half), half)
+        return pltpu.make_async_copy(
+            self.array.at[rows, self.columns],
+            self.acc.at[:, self.columns],
+            self.sems[2].at[self.index],
+        )
+
+    def empty(self):
+        size = self.size(self.halvings)
+        rows = pl.ds(pl.multiple_of(self.start(self.halvings), size), size)
+        to = pl.ds(pl.multiple_of(self.start(self.halvings, 0), size), size)
+        return pltpu.make_async_copy(
+            self.acc.at[rows, self.columns],
+            self.out.at[to, self.columns],
+            self.sems[3].at[self.index],
+        )
+
+    def begin(self):
+        self.fill().start()
+        self.copy(0).start()
+
+    def take(self, k):
+        self.copy(k).wait()
+        if k < len(self.order):
+            if k == 0:
+                self.fill().wait()
+            size = self.size(k + 1)
+            start = self.start(k + 1)
+            step = 16
+            base = self.base(k)
+
+            def add(i, carry):
+                r = pl.multiple_of(i * step, step)
+                mine = pl.ds(pl.multiple_of(start + r, step), step)
+                self.acc[mine, self.columns] = (
+                    self.acc[mine, self.columns] + self.recv[pl.ds(base + r, step), self.columns]
+                )
+                return carry
+
+            lax.fori_loop(0, size // step, add, 0)
+            if k == len(self.order) - 1:
+                self.empty().start()
+                self.empty().wait()
+        if k + 1 < self.waits:
+            self.copy(k + 1).start()
+
+
+def halvings_of(rows, stages):
+    count = 0
+    while count < stages - 1 and rows % (32 << count) == 0:
+        count += 1
+    return count
+
+
+def exchange_rows(rows, stages):
+    count = halvings_of(rows, stages)
+    return sum(rows >> min(s + 1, count) for s in range(stages))
 
 
 def attention_kernel(
     seqs,
     groups,
+    orders,
     q_ref,
     g_ref,
     all_ref,
+    down_ref,
+    up_ref,
     att_ref,
     dq_ref,
     slot_ref,
+    down_sum_ref,
+    up_sum_ref,
     kvt_ref,
     flat_ref,
     rows_ref,
@@ -179,6 +290,15 @@
     core_recv,
     slot_send,
     slot_recv,
+    down_acc_ref,
+    up_acc_ref,
+    down_recv_ref,
+    up_recv_ref,
+    graw_ref,
+    sum_send,
+    sum_recv,
+    fill_sem,
+    empty_sem,
 ):
     tiles, width, rows = q_ref.shape
     ring = all_ref.shape[0]
@@ -204,7 +324,12 @@
     greet(flip(me, 1))
     for m in range(1, chips):
         greet(lax.rem(me + 2 * m, ring))
-    pl.semaphore_wait(barrier, chips + 1)
+    across = [bit for bit in orders[0] if bit[0] == "dp"]
+    for bit in across:
+        pl.semaphore_signal(
+            barrier, inc=1, device_id=partner_of(bit), device_id_type=MESH
+        )
+    pl.semaphore_wait(barrier, chips + 1 + len(across))
 
     def load(s, slot):
         return pltpu.make_async_copy(
@@ -240,16 +365,67 @@
     def dq_out(k):
         return remote(dqs_ref.at[k], dq_ref.at[place(k)], (out_send, out_recv), 1, k, partner)
 
-    def start_in(k, carry):
-        q_in(k).start()
-        g_in(k).start()
+    def given_of(s):
+        return (count - s + seqs - 1) // seqs
+
+    def start_in(s):
+        def one(i, carry):
+            q_in(i * seqs + s).start()
+            g_in(i * seqs + s).start()
+            return carry
+
+        lax.fori_loop(0, upper * given_of(s), one, 0)
+
+    start_in(0)
+
+    sems = (sum_send, sum_recv, fill_sem, empty_sem)
+    half_down, half_up = down_ref.shape[1] // 2, up_ref.shape[1] // 2
+    teams = []
+    for i in range(2):
+        teams.append(
+            [
+                Exchange(
+                    2 * i, orders[0], down_ref, down_sum_ref, down_acc_ref, down_recv_ref,
+                    i * half_down, half_down, sems,
+                ),
+                Exchange(
+                    2 * i + 1, orders[1], up_ref, up_sum_ref, up_acc_ref, up_recv_ref,
+                    i * half_up, half_up, sems,
+                ),
+            ]
+        )
+    most_waits = [max(e.waits for e in team) for team in teams]
+    acts = sorted(
+        [(k + 0.75 * i, i, k) for i in range(2) for k in range(most_waits[i])]
+    )
+    acts = [(i, k) for _, i, k in acts]
+    for team in teams:
+        for e in team:
+            e.begin()
+
+    def act(number, carry):
+        for n, (i, k) in enumerate(acts):
+            def run(i=i, k=k):
+                for e in teams[i]:
+                    if k < e.waits:
+                        e.take(k)
+
+            pl.when(number == n)(run)
         return carry
 
-    lax.fori_loop(0, count * upper, start_in, 0)
+    def cost_of(position):
+        return position * rows // KEYS + 2
+
+    total_cost = (tiles - upper * count) * cost_of(me) + (1 - upper) * count * cost_of(partner)
+
+    def advance(acted, progress):
+        due = jnp.minimum(progress * (len(acts) + 1) // total_cost, len(acts))
+        lax.fori_loop(acted, due, act, 0)
+        return jnp.maximum(acted, due)
 
     def core_out(s):
         return pltpu.make_async_remote_copy(
-            src_ref=stage_ref.at[s, :, 1 - core],
+            src_ref=stage_ref.at[lax.rem(s, 2), :, 1 - core],
             dst_ref=half_ref.at[s],
             send_sem=core_send.at[s],
             recv_sem=core_recv.at[s],
@@ -272,11 +448,11 @@
         return pltpu.make_async_copy(half_ref.at[s, chip], slot_ref.at[s, 0], own_sem.at[s])
 
     def pass_on(s):
-        core_out(s).wait_recv()
+        core_out(s).wait()
 
         def add(m, carry):
             half_ref[s, m] = (
-                half_ref[s, m].astype(F32) + stage_ref[s, m, core].astype(F32)
+                half_ref[s, m].astype(F32) + stage_ref[lax.rem(s, 2), m, core].astype(F32)
             ).astype(BF)
             return carry
 
@@ -299,14 +475,36 @@
         )
         return lax.fori_loop(2 * pairs, count_blocks, lambda i, c: body(i, 1, c), state)
 
-    def tile(q_tile, g_tile, att_tile, dq_tile, position):
+    def spread(tile, out):
+        for h in range(heads):
+            tile[h * HEAD_DIM : (h + 1) * HEAD_DIM, :] = out[:, h * rows : (h + 1) * rows].astype(
+                BF
+            )
+
+    def gather(tile, out):
+        for h in range(heads):
+            out[0:HEAD_DIM, h * rows : (h + 1) * rows] = tile[
+                h * HEAD_DIM : (h + 1) * HEAD_DIM, :
+            ]
+
+    def tile(mine, t, k, position, acted, progress):
         start = position * rows
         edge = start // KEYS
         shift = lax.rem(start, KEYS)
-        for h in range(heads):
-            qs_ref[0:HEAD_DIM, h * rows : (h + 1) * rows] = q_tile[
-                h * HEAD_DIM : (h + 1) * HEAD_DIM, :
-            ]
+        other = jnp.logical_not(mine)
+
+        @pl.when(mine)
+        def _():
+            gather(q_ref.at[t], qs_ref)
+            gather(g_ref.at[t], graw_ref)
+
+        @pl.when(other)
+        def _():
+            q_in(k).wait_recv()
+            g_in(k).wait_recv()
+            gather(qin_ref.at[k], qs_ref)
+            gather(gin_ref.at[k], graw_ref)
+
         s = dot(rows_ref[at(edge), :], qs_ref[...], 1, 0)
         column = lax.rem(lax.broadcasted_iota(jnp.int32, (1, lanes), 1), rows) + shift
         keep = lax.broadcasted_iota(jnp.int32, (KEYS, lanes), 0) <= column
@@ -338,13 +536,15 @@
         )
         inverse = 1.0 / jnp.sum(total, axis=0, keepdims=True)
         out = out * inverse
-        for h in range(heads):
-            att_tile[h * HEAD_DIM : (h + 1) * HEAD_DIM, :] = out[
-                :, h * rows : (h + 1) * rows
-            ].astype(BF)
-        g = jnp.concatenate(
-            [g_tile[h * HEAD_DIM : (h + 1) * HEAD_DIM, :] for h in range(heads)], axis=1
-        )
+        pl.when(mine)(lambda: spread(att_ref.at[t], out))
+
+        @pl.when(other)
+        def _():
+            spread(atts_ref.at[k], out)
+            att_out(k).start()
+
+        acted = advance(acted, progress + (edge + 2) // 2)
+        g = graw_ref[...]
         scaled = (g.astype(F32) * inverse).astype(BF)
         gs_ref[HEAD_DIM : 2 * HEAD_DIM, :] = scaled
         delta = jnp.sum(scaled.astype(F32) * out, axis=0, keepdims=True)
@@ -358,14 +558,19 @@
 
         dq = blocks(edge + 1, backward, jnp.zeros((HEAD_DIM, lanes), F32))
         dq = dq * (HEAD_DIM**-0.5)
-        for h in range(heads):
-            dq_tile[h * HEAD_DIM : (h + 1) * HEAD_DIM, :] = dq[
-                :, h * rows : (h + 1) * rows
-            ].astype(BF)
+        pl.when(mine)(lambda: spread(dq_ref.at[t], dq))
+
+        @pl.when(other)
+        def _():
+            spread(dqs_ref.at[k], dq)
+            dq_out(k).start()
+
+        progress = progress + edge + 2
+        return advance(acted, progress), progress
 
     per_block = KEYS // rows
 
-    def sequence(s, carry):
+    def sequence(s, state):
         slot = lax.rem(s, 2)
         load(s, slot).wait()
         pl.when(s + 1 < seqs)(lambda: load(s + 1, 1 - slot).start())
@@ -380,39 +585,31 @@
             return c
 
         lax.fori_loop(0, length // KEYS, turn, 0)
-        given = (count - s + seqs - 1) // seqs
+        given = given_of(s)
         own = groups - upper * given
         taken = (1 - upper) * given
         later = jnp.minimum(s, 1)
 
-        def work(u, c):
+        def work(u, state):
+            acted, progress = state
             v = u - taken * later
             mine = (v >= 0) & (v < own)
-
-            @pl.when(mine)
-            def _():
-                t = s * groups + upper * given + v
-                tile(q_ref.at[t], g_ref.at[t], att_ref.at[t], dq_ref.at[t], me)
-
-            @pl.when(jnp.logical_not(mine))
-            def _():
-                k = (u - own * (1 - later)) * seqs + s
-                q_in(k).wait_recv()
-                g_in(k).wait_recv()
-                tile(qin_ref.at[k], gin_ref.at[k], atts_ref.at[k], dqs_ref.at[k], partner)
-                att_out(k).start()
-                dq_out(k).start()
-
+            t = s * groups + upper * given + jnp.clip(v, 0, own - 1)
+            k = jnp.clip(u - own * (1 - later), 0, jnp.maximum(taken - 1, 0)) * seqs + s
+            position = jnp.where(mine, me, partner)
+            state = tile(mine, t, k, position, acted, progress)
             pl.when((u == 0) & (s > 0))(lambda: pass_on(s - 1))
-            return c
-
-        lax.fori_loop(0, own + taken, work, 0)
-        stage_ref[s] = dkv_ref[...].reshape(chips, 2, rows, 2 * HEAD_DIM).astype(BF)
+            pl.when((u == 0) & (s + 1 < seqs))(lambda: start_in(s + 1))
+            return state
+
+        state = lax.fori_loop(0, own + taken, work, state)
+        stage_ref[slot] = dkv_ref[...].reshape(chips, 2, rows, 2 * HEAD_DIM).astype(BF)
         core_out(s).start()
-        return carry
-
-    lax.fori_loop(0, seqs, sequence, 0)
+        return state
+
+    acted, _ = lax.fori_loop(0, seqs, sequence, (jnp.int32(0), jnp.int32(0)))
     pass_on(seqs - 1)
+    lax.fori_loop(acted, len(acts), act, 0)
 
     def end_given(k, c):
         q_in(k).wait_send()
@@ -430,7 +627,6 @@
     lax.fori_loop(0, count * (1 - upper), end_taken, 0)
 
     def end(s, c):
-        core_out(s).wait_send()
         slot_own(s).wait()
         for m in range(1, chips):
             slot_out(s, m).wait()
@@ -439,7 +635,7 @@
     lax.fori_loop(0, seqs, end, 0)
 
 
-def attention(q, g, kv_all, seqs):
+def attention(q, g, kv_all, down, up, seqs, dp):
     tiles, width, rows = q.shape
     ring = kv_all.shape[0]
     chips = ring // 2
@@ -450,15 +646,19 @@
     anywhere = pl.BlockSpec(memory_space=pl.ANY)
     pair = 2 * HEAD_DIM
     dma = pltpu.SemaphoreType.DMA
+    orders = bit_orders(dp, ring)
+    stages = len(orders[0])
     return pl.pallas_call(
-        functools.partial(attention_kernel, seqs, tiles // seqs),
+        functools.partial(attention_kernel, seqs, tiles // seqs, orders),
         out_shape=[
             jax.ShapeDtypeStruct(q.shape, BF),
             jax.ShapeDtypeStruct(q.shape, BF),
             jax.ShapeDtypeStruct((seqs, chips, rows, pair), BF),
+            jax.ShapeDtypeStruct(down.shape, BF),
+            jax.ShapeDtypeStruct(up.shape, BF),
         ],
-        in_specs=[vmem, vmem, anywhere],
-        out_specs=[vmem, vmem, anywhere],
+        in_specs=[vmem, vmem, anywhere, anywhere, anywhere],
+        out_specs=[vmem, vmem, anywhere, anywhere, anywhere],
         scratch_shapes=[
             pltpu.VMEM((2, ring, pair, rows), BF),
             pltpu.VMEM((pair, length), BF),
@@ -472,7 +672,7 @@
             pltpu.VMEM((most, width, rows), BF),
             pltpu.VMEM((most, width, rows), BF),
             pltpu.VMEM((most, width, rows), BF),
-            pltpu.VMEM((seqs, chips, 2, rows, pair), BF),
+            pltpu.VMEM((2, chips, 2, rows, pair), BF),
             pltpu.VMEM((seqs, chips, rows, pair), BF),
             dma((2,)),
             dma((seqs,)),
@@ -484,9 +684,18 @@
             dma((seqs,)),
             dma((seqs, chips)),
             dma((seqs, chips)),
+            pltpu.VMEM((down.shape[0] // 2, down.shape[1]), BF),
+            pltpu.VMEM((up.shape[0] // 2, up.shape[1]), BF),
+            pltpu.VMEM((exchange_rows(down.shape[0], stages), down.shape[1]), BF),
+            pltpu.VMEM((exchange_rows(up.shape[0], stages), up.shape[1]), BF),
+            pltpu.VMEM((HEAD_DIM, lanes), BF),
+            dma((4, 2 * stages)),
+            dma((4, 2 * stages)),
+            dma((4,)),
+            dma((4,)),
         ],
         compiler_params=pltpu.CompilerParams(
-            collective_id=2, has_side_effects=True, vmem_limit_bytes=58 * 2**20
+            collective_id=2, has_side_effects=True, vmem_limit_bytes=60 * 2**20
         ),
         cost_estimate=pl.CostEstimate(
             flops=12 * tiles * rows * width * length * 4,
@@ -494,7 +703,7 @@
             transcendentals=tiles * lanes * length // 2,
         ),
         name="attention",
-    )(q, g, kv_all)
+    )(q, g, kv_all, down, up)
 
 
 def bit_orders(dp, ring):
@@ -665,12 +874,10 @@
     query_tiles, grad_tiles, kv_all, grad_w_up, grad_w_down = lax.optimization_barrier(
         (query_tiles, grad_tiles, kv_all, grad_w_up, grad_w_down)
     )
-    grad_w_down = lax.psum(grad_w_down, ("dp", "seq"))
-    out, dq, dkv = attention(query_tiles, grad_tiles, kv_all, seq_count)
-    out, dq, dkv, grad_w_up, grad_w_down = lax.optimization_barrier(
-        (out, dq, dkv, grad_w_up, grad_w_down)
-    )
-    grad_w_up = lax.psum(grad_w_up, ("dp", "seq"))
+    dp = lax.axis_size("dp")
+    out, dq, dkv, grad_w_down, grad_w_up = attention(
+        query_tiles, grad_tiles, kv_all, grad_w_down, grad_w_up, seq_count, dp
+    )
     attended = out.reshape(seq_count, D, local_len)
     query_back = dq.reshape(seq_count, HEADS, HEAD_DIM, local_len)
     kv_grad = jnp.sum(dkv.astype(F32), axis=1)
@@ -726,7 +933,6 @@
         axis=0,
     ).astype(BF)
     rest = total_of(rest, dp, ring, 3)
-    rest, grad_w_up = lax.optimization_barrier((rest, grad_w_up))
     rest = rest.astype(F32)
     vectors = rest[square // D :].reshape(-1)
     rest_kv = rest[2 * D : 2 * D + 2 * HEAD_DIM]

time: 511 us -> 420 us (0.82); the launches traced: 501 us -> 416 us
  waiting for transfers between devices: 89.4 us -> 0.02 us
    psum x2 -> x0, waiting for transfers between devices: 89.4 us -> none  [the longest x1 61.6 us: local(): grad_w_up = lax.psum(grad_w_up, ('dp', 'seq'))]
    pallas_call x1, Pallas kernels: 190 us -> 200 us  [attention(): pl.pallas_call(functools.partial(attention_kernel, seqs, tiles // seqs, o...]
    pallas_call x1, Pallas kernels: 65.2 us -> 58.7 us  [total_of(): pl.pallas_call(functools.partial(sum_kernel, orders), out_shape=jax.Shape...]
  transfers between devices with their start and end apart: 3 -> 1, of which waited for: 2 -> 0; matrix products, arithmetic and copies ran while one was open for 9% -> 7% of each run, Pallas kernels for 59% -> 10%
where the time goes in v4:
time: 420 us; the launch traced here: 416 us
  Pallas kernels  300 us (71%)
  other arithmetic  51.1 us (12%)
  local copies, waits for them, and re-layouts  25.7 us (6%)
  matrix products  24.1 us (6%)
  between operations  15 us (4%)
    pallas_call x1, Pallas kernels, attention(): pl.pallas_call(functools.partial(attention_kernel, seqs, tiles // seqs, o...  200 us
    pallas_call x1, Pallas kernels, total_of(): pl.pallas_call(functools.partial(sum_kernel, orders), out_shape=jax.Shape...  58.7 us
    pallas_call x1, Pallas kernels, feed_forward(): pl.pallas_call(feed_kernel, grid=(FEED_STEPS,), out_shape=[jax.ShapeDtype...  41.2 us
  transfers between devices with their start and end apart: 1, of which 0 were waited for; matrix products, arithmetic and copies ran while one was open for 7% of the time, Pallas kernels for 10%

profile of v4, /device:TPU:0, one launch (start us, length us, event | category | flops | bytes accessed | tf_op | source)
XLA Modules:
  0.0 416.4 jit_solution(18206537653291533764)
XLA Ops:
  7.4 1.8 convert_reduce_fusion
  9.2 2.0 fusion.16
  11.9 0.9 fusion.27
  12.9 0.8 fusion.43
  13.7 0.7 pad_maximum_fusion.3
  14.5 0.8 copy.70
  15.3 0.8 copy.71
  16.1 4.6 %add_bitcast_fusion = f32[4,768,256]{1,2,0:T(8,128)} fusion(f32[768]{0:T(1024)S(1)} %copy-done.51, bf16[768,768]{1,0:T(8,128)(2,1)} %param.25, bf16[4,256,768]{2,1,0:T(8,128)(2,1)S(1)} %copy-done.4, f32[768]{0:T(1024)S(1)} %copy-done.52, f32[768]{0:T(1024)S(1)} %copy-done.32, f32[4,256]{1,0:T(4,128)S(1)} %fusion.54, f32[4,256]{1,0:T(4,128)S(1)} %broadcast_multiply_fusion), kind=kOutput, calls=%fused_computation.30 | convolution fusion | flops 1213464576 | bytes 5915648 | tf_op jit(solution)/shard_map/stc,cw->swt/dot_general | solution.py:854
  20.7 4.0 copy.63
  24.8 3.4 slice.163
  28.1 2.3 reduce.2
  30.4 1.8 fusion.13
  32.2 41.2 %feed_forward.1 = (f32[1024,768]{1,0:T(8,128)}, f32[1024,768]{1,0:T(8,128)}, bf16[768,3072]{1,0:T(8,128)(2,1)}, bf16[3072,768]{1,0:T(8,128)(2,1)}, f32[1,3072]{1,0:T(1,128)}) custom-call(bf16[1024,768]{1,0:T(8,128)(2,1)} %bitcast.61, bf16[1024,768]{1,0:T(8,128)(2,1)} %bitcast.57, bf16[768,3072]{1,0:T(8,128)(2,1)} %up_ref.1, bf16[3072,768]{1,0:T(8,128)(2,1)} %down_ref.1, ...), custom_call_target="tpu_custom_call" | custom-call | flops 28991029248 | bytes 37748736 | tf_op jit(solution)/shard_map/feed_forward/pallas_call | solution.py:118
  73.4 2.9 reduce_sum.132
  76.3 1.3 add.103
  77.6 0.6 convert_reduce_fusion.2
  78.2 1.3 multiply_subtract_fusion
  79.5 1.6 fusion.21
  81.1 2.6 convolution_convert_fusion
  83.7 200.4 %attention.1 = (bf16[16,192,256]{2,1,0:T(8,128)(2,1)}, bf16[16,192,256]{2,1,0:T(8,128)(2,1)}, bf16[4,8,256,128]{3,2,1,0:T(8,128)(2,1)}, bf16[3072,768]{1,0:T(8,128)(2,1)}, bf16[768,3072]{1,0:T(8,128)(2,1)}) custom-call(bf16[16,192,256]{2,1,0:T(8,128)(2,1)} %bitcast.62, bf16[16,192,256]{2,1,0:T(8,128)(2,1)} %bitcast.68, ...), custom_call_target="tpu_custom_call" | custom-call | flops 154618822656 | bytes 6291456 | tf_op jit(solution)/shard_map/attention/pallas_call | solution.py:651
  284.1 1.9 convert_element_type.101
  286.4 1.6 copy.66
  288.0 2.8 convert_reduce_fusion.1
  290.9 1.2 copy.65
  292.1 0.9 fusion.59
  293.3 1.6 fusion.51
  295.0 0.9 copy.68
  296.0 3.5 bitcast_convert_fusion
  299.5 1.1 slice.173
  300.6 0.7 slice_bitcast_fusion.2
  301.4 1.1 fusion.57
  302.5 2.4 copy.75
  304.8 5.9 %fusion.58 = (bf16[768]{0:T(1024)(128)(2,1)}, f32[4,256]{1,0:T(4,128)S(1)}, f32[4,256]{1,0:T(4,128)S(1)}, f32[4,256,768]{2,1,0:T(8,128)S(1)}) fusion(f32[768]{0:T(1024)S(1)} %copy-done.33, f32[4,256]{1,0:T(4,128)S(1)} %copy-done.18, bf16[4,256,768]{2,1,0:T(8,128)(2,1)S(1)} %copy-done.5, f32[4,256,768]{2,1,0:T(8,128)} %bitcast.53, f32[768]{0:T(1024)S(1)} %copy-done.24, ...), kind=kOutput, calls=%fused_computation.100 | convolution fusion | flops 1427830016 | bytes 11095552 | tf_op jit(solution)/shard_map/swt,cw->stc/dot_general | solution.py:905
  310.8 3.1 fusion.14
  315.8 3.4 bitcast_convert_fusion.1
  319.2 1.9 pad_maximum_fusion.x_ref
  321.1 58.7 %total.1 = bf16[1792,768]{1,0:T(8,128)(2,1)} custom-call(bf16[1792,768]{1,0:T(8,128)(2,1)} %pad_maximum_fusion.x_ref), custom_call_target="tpu_custom_call" | custom-call | tf_op jit(solution)/shard_map/total/pallas_call | solution.py:804
  379.9 2.3 convert_element_type.108
  382.2 0.8 slice_bitcast_fusion
  383.0 0.6 slice_reduce_fusion
  383.7 2.5 fusion.61
  386.3 0.6 slice.188
  386.9 0.6 fusion.62
  387.5 7.4 %convert_element_type.109 = f32[768,3072]{1,0:T(8,128)} convert(bf16[768,3072]{1,0:T(8,128)(2,1)} %get-tuple-element.46) | non-fusion elementwise | flops 2359296 | bytes 14155776 | tf_op jit(solution)/shard_map/convert_element_type | solution.py:959
  394.9 7.0 %convert_element_type.110 = f32[3072,768]{1,0:T(8,128)} convert(bf16[3072,768]{1,0:T(8,128)(2,1)} %get-tuple-element.47) | non-fusion elementwise | flops 2359296 | bytes 14155776 | tf_op jit(solution)/shard_map/convert_element_type | solution.py:961
  401.9 3.4 add_add_fusion.2
  405.3 3.3 fusion.20
  408.7 0.6 copy.89
  (144 shorter events, 3.6 us)
Async XLA Ops:
  7.2 73.9 %copy-start = (bf16[768,768]{1,0:T(8,128)(2,1)S(1)}, bf16[768,768]{1,0:T(8,128)(2,1)}, u32[]{:S(2)}) copy-start(bf16[768,768]{1,0:T(8,128)(2,1)} %param.31) | copy-start | bytes 3538948
  7.2 4.7 %copy-start.4 = (bf16[4,256,768]{2,1,0:T(8,128)(2,1)S(1)}, bf16[4,256,768]{2,1,0:T(8,128)(2,1)}, u32[]{:S(2)}) copy-start(bf16[4,256,768]{2,1,0:T(8,128)(2,1)} %param.19) | copy-start | bytes 4718596
  7.2 4.0 copy-start.47
  7.2 4.6 %copy-start.54 = (f32[64]{0:T(128)S(1)}, f32[64]{0:T(128)}, u32[]{:S(2)}) copy-start(f32[64]{0:T(128)} %param.28) | copy-start | bytes 772
  7.2 4.6 %copy-start.53 = (f32[64]{0:T(128)S(1)}, f32[64]{0:T(128)}, u32[]{:S(2)}) copy-start(f32[64]{0:T(128)} %param.30) | copy-start | bytes 772
  7.2 4.7 %copy-start.32 = (f32[768]{0:T(1024)S(1)}, f32[768]{0:T(1024)}, u32[]{:S(2)}) copy-start(f32[768]{0:T(1024)} %param.21) | copy-start | bytes 9220
  7.3 4.6 %copy-start.52 = (f32[768]{0:T(1024)S(1)}, f32[768]{0:T(1024)}, u32[]{:S(2)}) copy-start(f32[768]{0:T(1024)} %param.22) | copy-start | bytes 9220
  7.3 4.6 %copy-start.19 = (bf16[768,64]{0,1:T(8,128)(2,1)S(1)}, bf16[768,64]{0,1:T(8,128)(2,1)}, u32[]{:S(2)}) copy-start(bf16[768,64]{0,1:T(8,128)(2,1)} %param.27) | copy-start | bytes 294916
  7.3 4.6 %copy-start.20 = (bf16[768,64]{0,1:T(8,128)(2,1)S(1)}, bf16[768,64]{0,1:T(8,128)(2,1)}, u32[]{:S(2)}) copy-start(bf16[768,64]{0,1:T(8,128)(2,1)} %param.29) | copy-start | bytes 294916
  7.3 76.4 %all-gather.2.cloned.1.call-start = ((), (), s32[]{:S(2)}) async-start(), calls=%async_computation | async-start | bytes 4456448 | tf_op jit(solution)/shard_map/all_gather | solution.py:853
  7.4 5.5 %copy-start.48 = (f32[8]{0:T(128)}, f32[8]{0:T(128)S(1)}, u32[]{:S(2)}) copy-start(f32[8]{0:T(128)S(1)} %multiply_exponential_fusion) | copy-start | bytes 100
  9.2 21.2 %copy-start.17 = (f32[4,256]{1,0:T(4,128)}, f32[4,256]{1,0:T(4,128)S(1)}, u32[]{:S(2)}) copy-start(f32[4,256]{1,0:T(4,128)S(1)} %broadcast_multiply_fusion) | copy-start | bytes 12292
  11.2 19.2 %copy-start.21 = (f32[4,256]{1,0:T(4,128)}, f32[4,256]{1,0:T(4,128)S(1)}, u32[]{:S(2)}) copy-start(f32[4,256]{1,0:T(4,128)S(1)} %fusion.54) | copy-start | bytes 12292
  11.9 4.2 %copy-start.51 = (f32[768]{0:T(1024)S(1)}, f32[768]{0:T(1024)}, u32[]{:S(2)}) copy-start(f32[768]{0:T(1024)} %param.26) | copy-start | bytes 9220
  24.8 5.7 %copy-start.23 = (f32[768]{0:T(1024)S(1)}, f32[768]{0:T(1024)}, u32[]{:S(2)}) copy-start(f32[768]{0:T(1024)} %param.23) | copy-start | bytes 9220
  24.8 5.7 %copy-start.44 = (f32[768]{0:T(1024)S(1)}, f32[768]{0:T(1024)}, u32[]{:S(2)}) copy-start(f32[768]{0:T(1024)} %param.24) | copy-start | bytes 9220
  73.4 4.2 %copy-start.40 = (f32[1,3072]{1,0:T(1,128)S(1)}, f32[1,3072]{1,0:T(1,128)}, u32[]{:S(2)}) copy-start(f32[1,3072]{1,0:T(1,128)} %get-tuple-element.45) | copy-start | bytes 36868
  73.4 6.1 %copy-start.8 = (f32[4,12,48,256]{3,2,1,0:T(8,128)S(1)}, f32[4,12,48,256]{3,2,1,0:T(8,128)}, u32[]{:S(2)}) copy-start(f32[4,12,48,256]{3,2,1,0:T(8,128)} %slice.163) | copy-start | bytes 7077892
  286.4 5.7 %copy-start.50 = (f32[128]{0:T(128)S(1)}, f32[128]{0:T(128)}, u32[]{:S(2)}) copy-start(f32[128]{0:T(128)} %constant.22.clone.1) | copy-start | bytes 1540
  288.0 5.2 %copy-start.30 = (f32[4,256]{1,0:T(4,128)S(1)}, f32[4,256]{1,0:T(4,128)}, u32[]{:S(2)}) copy-start(f32[4,256]{1,0:T(4,128)} %copy-done.29) | copy-start | bytes 12292
  288.0 7.9 %copy-start.5 = (bf16[4,256,768]{2,1,0:T(8,128)(2,1)S(1)}, bf16[4,256,768]{2,1,0:T(8,128)(2,1)}, u32[]{:S(2)}) copy-start(bf16[4,256,768]{2,1,0:T(8,128)(2,1)} %param.19) | copy-start | bytes 4718596
  288.0 7.9 %copy-start.18 = (f32[4,256]{1,0:T(4,128)S(1)}, f32[4,256]{1,0:T(4,128)}, u32[]{:S(2)}) copy-start(f32[4,256]{1,0:T(4,128)} %copy-done.17) | copy-start | bytes 12292
  288.0 7.9 %copy-start.22 = (f32[4,256]{1,0:T(4,128)S(1)}, f32[4,256]{1,0:T(4,128)}, u32[]{:S(2)}) copy-start(f32[4,256]{1,0:T(4,128)} %copy-done.21) | copy-start | bytes 12292
  288.0 7.9 %copy-start.33 = (f32[768]{0:T(1024)S(1)}, f32[768]{0:T(1024)}, u32[]{:S(2)}) copy-start(f32[768]{0:T(1024)} %param.21) | copy-start | bytes 9220
  300.6 4.2 %copy-start.24 = (f32[768]{0:T(1024)S(1)}, f32[768]{0:T(1024)}, u32[]{:S(2)}) copy-start(f32[768]{0:T(1024)} %param.23) | copy-start | bytes 9220
  304.8 5.9 %copy-start.28 = (f32[4,256]{1,0:T(4,128)S(1)}, f32[4,256]{1,0:T(4,128)}, u32[]{:S(2)}) copy-start(f32[4,256]{1,0:T(4,128)} %copy-done.27) | copy-start | bytes 12292
  304.8 5.9 %copy-start.1 = (f32[1024,768]{1,0:T(8,128)S(1)}, f32[1024,768]{1,0:T(8,128)}, u32[]{:S(2)}) copy-start(f32[1024,768]{1,0:T(8,128)} %get-tuple-element.44) | copy-start | bytes 9437188
  304.8 5.9 %copy-start.34 = (f32[768]{0:T(1024)S(1)}, f32[768]{0:T(1024)}, u32[]{:S(2)}) copy-start(f32[768]{0:T(1024)} %param.21) | copy-start | bytes 9220
  310.7 3.3 copy-start.6
  310.8 3.4 copy-start.49
  310.8 3.8 copy-start.42
  310.8 4.0 copy-start.43
  310.8 4.2 %copy-start.31 = (bf16[3072]{0:T(1024)(128)(2,1)S(1)}, bf16[3072]{0:T(1024)(128)(2,1)}, u32[]{:S(2)}) copy-start(bf16[3072]{0:T(1024)(128)(2,1)} %convert_reduce_fusion.2) | copy-start | bytes 18436
  310.8 4.5 %copy-start.41 = (bf16[768]{0:T(1024)(128)(2,1)S(1)}, bf16[768]{0:T(1024)(128)(2,1)}, u32[]{:S(2)}) copy-start(bf16[768]{0:T(1024)(128)(2,1)} %reduce.2) | copy-start | bytes 4612
  315.8 3.4 copy-start.13
  315.8 3.4 copy-start.14
  379.9 3.8 copy-start.3
  386.9 21.8 %copy-start.38 = (f32[768]{0:T(1024)}, f32[768]{0:T(1024)S(1)}, u32[]{:S(2)}) copy-start(f32[768]{0:T(1024)S(1)} %slice.187) | copy-start | bytes 9220
  394.8 7.0 %copy-start.36 = (f32[4,256]{1,0:T(4,128)S(1)}, f32[4,256]{1,0:T(4,128)}, u32[]{:S(2)}) copy-start(f32[4,256]{1,0:T(4,128)} %get-tuple-element.54) | copy-start | bytes 12292
  394.8 7.0 %copy-start.37 = (f32[4,256]{1,0:T(4,128)S(1)}, f32[4,256]{1,0:T(4,128)}, u32[]{:S(2)}) copy-start(f32[4,256]{1,0:T(4,128)} %get-tuple-element.58) | copy-start | bytes 12292
  394.8 7.0 %copy-start.2 = (f32[1024,768]{1,0:T(8,128)S(1)}, f32[1024,768]{1,0:T(8,128)}, u32[]{:S(2)}) copy-start(f32[1024,768]{1,0:T(8,128)} %get-tuple-element.44) | copy-start | bytes 9437188
  394.8 7.0 %copy-start.7 = (f32[4,256,768]{2,1,0:T(8,128)S(1)}, f32[4,256,768]{2,1,0:T(8,128)}, u32[]{:S(2)}) copy-start(f32[4,256,768]{2,1,0:T(8,128)} %copy-done.6) | copy-start | bytes 9437188
  394.8 7.0 %copy-start.10 = (bf16[4,256,768]{2,1,0:T(8,128)(2,1)S(1)}, bf16[4,256,768]{2,1,0:T(8,128)(2,1)}, u32[]{:S(2)}) copy-start(bf16[4,256,768]{2,1,0:T(8,128)(2,1)} %param.37) | copy-start | bytes 4718596
  394.9 7.0 %copy-start.26 = (f32[4,256]{1,0:T(4,128)S(1)}, f32[4,256]{1,0:T(4,128)}, u32[]{:S(2)}) copy-start(f32[4,256]{1,0:T(4,128)} %copy-done.25) | copy-start | bytes 12292
  394.9 7.0 %copy-start.35 = (f32[768]{0:T(1024)S(1)}, f32[768]{0:T(1024)}, u32[]{:S(2)}) copy-start(f32[768]{0:T(1024)} %param.21) | copy-start | bytes 9220
  401.9 3.4 copy-start.46
  401.9 3.4 copy-start.55
  401.9 3.4 copy-start.56
  (10 other events, 23.4 us)
Sparse Core Ops, SparseCore 0:
  14.6 53.4 all-gather.1
